TPU v7x, 256 devices: a whole 4x4x8 slice. The times are simulated.
256 devices in a mesh: cluster: 256 (over x, y, z, core).
Axes of the slice: x: 4, y: 4, z: 8, core: 2. Of those that a mesh axis runs over, the one named last changes fastest.
Arguments:
- x_block: float32 [8, 131072], P(None, 'cluster'), may hold values from -6 to 6
- near_tiles: float32 [2048, 27, 64, 64], P('cluster'), may hold values from -0.15625 to 0.15625
- near_list: int32 [2048, 27], P('cluster'), may hold values from 0 to 2047, as said below
- near_count: int32 [2048], P('cluster'), may hold values from 1 to 27, as said below
- leaf_in: float32 [2048, 64, 32], P('cluster'), may hold values from -0.75 to 0.75
- leaf_up: float32 [2048, 32, 32], P('cluster'), may hold values from -0.375 to 0.375
- mid_up: float32 [256, 32, 32], P('cluster'), may hold values from -0.375 to 0.375
- leaf_tiles: float32 [2048, 48, 32, 32], P('cluster'), may hold values from -0.21875 to 0.21875
- leaf_list: int32 [2048, 48], P('cluster'), may hold values from 0 to 2047, as said below
- leaf_count: int32 [2048], P('cluster'), may hold values from 1 to 48, as said below
- mid_tiles: float32 [256, 48, 32, 32], P('cluster'), may hold values from -0.21875 to 0.21875
- mid_list: int32 [256, 48], P('cluster'), may hold values from 0 to 255, as said below
- mid_count: int32 [256], P('cluster'), may hold values from 1 to 48, as said below
- top_tiles: float32 [32, 16, 32, 32], replicated, may hold values from -0.25 to 0.25
- top_list: int32 [32, 16], replicated, may hold values from 0 to 31
- mid_down: float32 [256, 32, 32], P('cluster'), may hold values from -1 to 1
- leaf_down: float32 [2048, 32, 32], P('cluster'), may hold values from -1 to 1
- leaf_out: float32 [2048, 64, 32], P('cluster'), may hold values from -0.75 to 0.75
Outputs:
- product: float32 [8, 131072], P(None, 'cluster')
Inputs may be any that keep to these rules, and one draw needn't show every extreme that they name: `near_list`: slot 0 is the leaf itself; every source leaf lies among the leaves of the target's own device block of 8 leaves and the blocks just before and after it. `near_count`: at least 1; the largest count is reached on some leaf. `leaf_list`: sources may be any leaf. `leaf_count`: loads differ from device to device; the largest count is reached on some leaf. `mid_list`: sources may be any middle cluster. `mid_count`: the largest count is reached on some middle cluster.
All inputs are finite; a program needn't handle non-finite values.
Results may differ from a plain program's by a relative error of at most 0.000061.
Values sent between devices are 32-bit elements; how exact they have to be, the bound alone decides.
A program may use at most 128 MiB of HBM per device.

v0:
```python
import jax
import jax.numpy as jnp
from jax import lax
from jax.sharding import PartitionSpec as P

HIGH = lax.Precision.HIGHEST


def with_halo(block, sides, width):
    for axis, dim in sides:
        count = lax.axis_size(axis)
        forward = [(i, i + 1) for i in range(count - 1)]
        backward = [(target, source) for source, target in forward]
        low = lax.ppermute(
            lax.slice_in_dim(block, block.shape[dim] - width, None, axis=dim), axis, forward
        )
        high = lax.ppermute(lax.slice_in_dim(block, 0, width, axis=dim), axis, backward)
        block = jnp.concatenate([low, block, high], axis=dim)
    return block


def couple_add(tiles, sources, live, piece, start):
    rows = piece.shape[0]
    local_idx = sources - start
    inside = (local_idx >= 0) & (local_idx < rows) & live
    picked = piece[jnp.clip(local_idx, 0, rows - 1)]
    return jnp.einsum(
        "ljca,ljcr,lj->lar", tiles, picked, inside.astype(jnp.float32), precision=HIGH
    )


def on_device(
    x_block,
    near_tiles,
    near_list,
    near_count,
    leaf_in,
    leaf_up,
    mid_up,
    leaf_tiles,
    leaf_list,
    leaf_count,
    mid_tiles,
    mid_list,
    mid_count,
    top_tiles,
    top_list,
    mid_down,
    leaf_down,
    leaf_out,
):
    nrhs, width = x_block.shape
    leaf_rows, panel, rank = leaf_in.shape
    mid_rows = mid_up.shape[0]
    top_rows = top_tiles.shape[0]
    devices = lax.axis_size("cluster")
    myself = lax.axis_index("cluster")
    padded = with_halo(x_block, (("cluster", 1),), width)
    extended = padded.reshape(nrhs, 3 * leaf_rows, panel)
    near_idx = near_list - (myself * leaf_rows - leaf_rows)
    near_live = (jnp.arange(near_list.shape[1])[None, :] < near_count[:, None]).astype(jnp.float32)
    picked = extended[:, near_idx]
    near = jnp.einsum("lnpq,rlnp,ln->rlq", near_tiles, picked, near_live, precision=HIGH)
    xl = x_block.reshape(nrhs, leaf_rows, panel)
    leaf_coef = jnp.einsum("lpa,rlp->lar", leaf_in, xl, precision=HIGH)
    mid_coef = (
        jnp.einsum("lab,lar->lbr", leaf_up, leaf_coef, precision=HIGH)
        .reshape(mid_rows, 8, rank, nrhs)
        .sum(1)
    )
    share = jnp.einsum("mab,mar->br", mid_up, mid_coef, precision=HIGH)
    mine = myself * mid_rows // 8
    shares = lax.all_gather(share[None], "cluster", axis=0, tiled=True)
    top_coef = shares.reshape(top_rows, devices // top_rows, rank, nrhs).sum(1)
    my_tiles = lax.dynamic_index_in_dim(top_tiles, mine, 0, keepdims=False)
    my_list = lax.dynamic_index_in_dim(top_list, mine, 0, keepdims=False)
    top_field = jnp.einsum("jab,jar->br", my_tiles, top_coef[my_list], precision=HIGH)
    leaf_live = jnp.arange(leaf_list.shape[1])[None, :] < leaf_count[:, None]
    mid_live = jnp.arange(mid_list.shape[1])[None, :] < mid_count[:, None]
    every_coef = lax.all_gather(leaf_coef, "cluster", axis=0, tiled=True)
    leaf_far = couple_add(leaf_tiles, leaf_list, leaf_live, every_coef, 0)
    every_mid = lax.all_gather(mid_coef, "cluster", axis=0, tiled=True)
    mid_far = couple_add(mid_tiles, mid_list, mid_live, every_mid, 0)
    mid_field = mid_far + jnp.einsum("mab,br->mar", mid_down, top_field, precision=HIGH)
    leaf_field = leaf_far + jnp.einsum(
        "lab,lbr->lar", leaf_down, jnp.repeat(mid_field, 8, axis=0), precision=HIGH
    )
    far = jnp.einsum("lpa,lar->rlp", leaf_out, leaf_field, precision=HIGH)
    return (near + far).reshape(nrhs, width)


def solution(mesh):
    placed = (
        P(None, "cluster"),
        P("cluster", None, None, None),
        P("cluster", None),
        P("cluster"),
        P("cluster", None, None),
        P("cluster", None, None),
        P("cluster", None, None),
        P("cluster", None, None, None),
        P("cluster", None),
        P("cluster"),
        P("cluster", None, None, None),
        P("cluster", None),
        P("cluster"),
        P(),
        P(),
        P("cluster", None, None),
        P("cluster", None, None),
        P("cluster", None, None),
    )
    return jax.shard_map(
        on_device, mesh=mesh, in_specs=placed, out_specs=P(None, "cluster"), check_vma=False
    )
```

profile of v0, /device:TPU:1, one launch (start us, length us, event | category | flops | bytes accessed | tf_op | source)
XLA Modules:
  0.0 193.6 jit_solution(18247083483667667079)
XLA Ops:
  6.5 0.0 copy-start
  6.5 0.0 copy-start.4
  6.5 0.0 copy-start.7
  6.5 0.0 copy-start.5
  6.5 0.0 copy-start.6
  6.5 0.0 copy-start.3
  6.6 0.0 all-gather.6.cloned.1.call-start
  6.6 0.8 reshape.86
  7.4 1.8 fusion.14
  9.3 0.0 all-gather.6.cloned.1.call-update
  9.3 4.9 %collective-permute-start = (f32[8,512]{1,0:T(8,128)}, f32[8,512]{1,0:T(8,128)S(1)}, u32[]{:S(2)}, u32[]{:S(2)}) collective-permute-start(f32[8,512]{1,0:T(8,128)} %param.18), channel_id=1, source_target_pairs={{0,1},{1,2},{2,3},{3,4},{4,5},{5,6},{6,7},{7,8},{8,9},{9,10},{10,1... | collective-permute-start | bytes 49160 | tf_op jit(solution)/shard_map/ppermute | solution.py:14
  14.2 1.9 collective-permute-start.1
  16.2 1.7 copy.38
  18.6 0.7 compare_select_fusion
  19.3 0.1 reshape.106
  19.4 0.7 compare_select_fusion.1
  20.1 0.1 reshape.98
  20.2 0.9 dynamic-slice_reduce_fusion
  21.1 1.2 fusion.27
  22.2 0.9 convolution_bitcast_fusion.2
  23.1 67.3 %all-gather.3 = f32[256,32,8]{1,2,0:T(8,128)S(1)} all-gather(f32[1,32,8]{1,2,0:T(8,128)S(1)} %convolution_bitcast_fusion.2), channel_id=3, replica_groups=mesh['cluster'=256] {'cluster'}, dimensions={0}, use_global_device_ids=true | all-gather | bytes 263168 | tf_op jit(solution)/shard_map/all_gather | solution.py:73
  90.4 0.1 bitcast_reduce_fusion
  90.5 0.6 gather_fusion.3
  91.1 0.7 fusion.23
  91.7 60.4 %all-gather.2 = f32[256,32,8]{1,2,0:T(8,128)S(1)} all-gather(f32[1,32,8]{1,2,0:T(8,128)S(1)} %bitcast.63), channel_id=2, replica_groups=mesh['cluster'=256] {'cluster'}, dimensions={0}, use_global_device_ids=true | all-gather | bytes 263168 | tf_op jit(solution)/shard_map/all_gather | solution.py:82
  152.2 0.6 gather_fusion.2
  152.8 0.0 copy-start.2
  152.8 1.2 convolution_bitcast_fusion.1
  154.1 0.0 copy-done.7
  154.1 1.3 convolution_bitcast_fusion.3
  155.3 0.0 copy-done.5
  155.3 0.1 fusion.20
  155.4 0.0 copy-done.4
  155.4 0.0 copy-done.6
  155.4 0.1 fusion.22
  155.5 0.0 copy-done.3
  155.5 0.1 fusion.6
  155.7 7.7 %copy.37 = f32[8,48,32,32]{3,2,1,0:T(8,128)} copy(f32[8,48,32,32]{1,3,2,0:T(8,128)} %param.25) | data formatting | bytes 3145728 | tf_op args[7]
  163.3 0.0 collective-permute-done
  163.4 0.0 collective-permute-done.1
  163.4 0.0 copy-done.2
  163.4 0.1 reshape.85
  163.5 0.9 gather_fusion
  164.4 6.5 %convolution_bitcast_fusion = f32[8,8,64]{2,1,0:T(8,128)S(1)} fusion(f32[8,27,64,64]{3,2,1,0:T(8,128)} %param.19, f32[8,27,8,64]{3,2,1,0:T(8,128)S(1)} %bitcast.61, f32[8,27]{1,0:T(8,128)S(1)} %fusion.20), kind=kOutput, calls=%fused_computation.10 | convolution fusion | flops 85045248 | bytes 3998560 | tf_op jit(solution)/shard_map/lnpq,rlnp,ln->rlq/dot_general | solution.py:63
  170.9 0.0 all-gather.6.cloned.1.call-done
  170.9 4.2 %gather_fusion.1 = f32[384,32,8]{1,2,0:T(8,128)S(1)} fusion(f32[2048,32,8]{1,2,0:T(8,128)} %all-gather.6.cloned.1.call-done, s32[1024]{0:T(1024)S(1)} %pad_clamp_fusion.2), kind=kCustom, calls=%fused_computation.1 | custom fusion | bytes 787968 | tf_op jit(solution)/shard_map/gather | solution.py:26
  175.2 0.0 copy-start.1
  175.2 10.2 %fusion.2 = f32[8,8,32]{2,1,0:T(8,128)S(1)} fusion(f32[8,48,32,32]{3,2,1,0:T(8,128)} %copy.37, f32[8,48,32,8]{2,3,1,0:T(8,128)S(1)} %bitcast.60, f32[8,48]{1,0:T(8,128)S(1)} %fusion.22), kind=kOutput, calls=%fused_computation.6 | convolution fusion | flops 37847040 | bytes 1975808 | tf_op jit(solution)/shard_map/ljca,ljcr,lj->lar/dot_general | solution.py:27
  185.4 0.0 copy-done.1
  185.4 0.3 convolution_add_fusion.1
  185.8 0.0 copy-done
  185.8 0.2 fusion.5
  186.0 0.7 reshape.94
  (9 shorter events, 0.1 us)
Async XLA Ops:
  6.5 179.2 %copy-start = (f32[8,64,32]{1,2,0:T(8,128)S(1)}, f32[8,64,32]{1,2,0:T(8,128)}, u32[]{:S(2)}) copy-start(f32[8,64,32]{1,2,0:T(8,128)} %param.35) | copy-start | bytes 196612
  6.5 148.9 %copy-start.4 = (s32[8,48]{1,0:T(8,128)S(1)}, s32[8,48]{1,0:T(8,128)}, u32[]{:S(2)}) copy-start(s32[8,48]{1,0:T(8,128)} %param.26) | copy-start | bytes 4612
  6.5 147.5 %copy-start.7 = (s32[1,48]{1,0:T(1,128)S(1)}, s32[1,48]{1,0:T(1,128)}, u32[]{:S(2)}) copy-start(s32[1,48]{1,0:T(1,128)} %param.29) | copy-start | bytes 580
  6.5 148.8 %copy-start.5 = (s32[8]{0:T(128)S(1)}, s32[8]{0:T(128)}, u32[]{:S(2)}) copy-start(s32[8]{0:T(128)} %param.21) | copy-start | bytes 100
  6.5 148.9 %copy-start.6 = (s32[8]{0:T(128)S(1)}, s32[8]{0:T(128)}, u32[]{:S(2)}) copy-start(s32[8]{0:T(128)} %param.27) | copy-start | bytes 100
  6.5 148.9 %copy-start.3 = (f32[1,32,32]{2,1,0:T(8,128)S(1)}, f32[1,32,32]{2,1,0:T(8,128)}, u32[]{:S(2)}) copy-start(f32[1,32,32]{2,1,0:T(8,128)} %param.33) | copy-start | bytes 12292
  6.6 164.4 %all-gather.6.cloned.1.call-start = ((), (), s32[]{:S(2)}) async-start(), calls=%async_computation | async-start | bytes 8421376 | tf_op jit(solution)/shard_map/all_gather | solution.py:80
  9.3 154.1 %collective-permute-start = (f32[8,512]{1,0:T(8,128)}, f32[8,512]{1,0:T(8,128)S(1)}, u32[]{:S(2)}, u32[]{:S(2)}) collective-permute-start(f32[8,512]{1,0:T(8,128)} %param.18), channel_id=1, source_target_pairs={{0,1},{1,2},{2,3},{3,4},{4,5},{5,6},{6,7},{7,8},{8,9},{9,10},{10,1... | collective-permute-start | bytes 49160 | tf_op jit(solution)/shard_map/ppermute | solution.py:14
  14.2 149.1 %collective-permute-start.1 = (f32[8,512]{1,0:T(8,128)}, f32[8,512]{1,0:T(8,128)S(1)}, u32[]{:S(2)}, u32[]{:S(2)}) collective-permute-start(f32[8,512]{1,0:T(8,128)} %param.18), channel_id=1, source_target_pairs={{1,0},{2,1},{3,2},{4,3},{5,4},{6,5},{7,6},{8,7},{9,8},{10,9},{11,1... | collective-permute-start | bytes 49160 | tf_op jit(solution)/shard_map/ppermute | solution.py:17
  152.8 10.6 %copy-start.2 = (f32[8,512]{1,0:T(8,128)S(1)}, f32[8,512]{1,0:T(8,128)}, u32[]{:S(2)}) copy-start(f32[8,512]{1,0:T(8,128)} %param.18) | copy-start | bytes 49156
  175.2 10.3 %copy-start.1 = (f32[8,32,32]{2,1,0:T(8,128)S(1)}, f32[8,32,32]{2,1,0:T(8,128)}, u32[]{:S(2)}) copy-start(f32[8,32,32]{2,1,0:T(8,128)} %param.34) | copy-start | bytes 98308
Sparse Core Ops, SparseCore 0:
  11.1 122.7 all-gather.5
where the time goes:
time: 194 us
  blocking collectives  128 us (66%)
  matrix products  23.8 us (12%)
  local copies, waits for them, and re-layouts  18.5 us (10%)
  between operations  14.3 us (7%)
  starting transfers between devices  6.9 us (4%)
  other arithmetic  2.34 us (1%)
    all_gather x1, blocking collectives, on_device(): shares = lax.all_gather(share[None], 'cluster', axis=0, tiled=True)  67.3 us
    all_gather x1, blocking collectives, on_device(): every_mid = lax.all_gather(mid_coef, 'cluster', axis=0, tiled=True)  60.4 us
    dot_general x2, matrix products, couple_add(): jnp.einsum('ljca,ljcr,lj->lar', tiles, picked, inside.astype(jnp.float32)...  11.5 us
    unnamed x17, local copies, waits for them, and re-layouts  7.73 us
    dot_general x1, matrix products, on_device(): jnp.einsum('lnpq,rlnp,ln->rlq', near_tiles, picked, near_live, precision=...  6.47 us
    ppermute x1, starting transfers between devices, with_halo(): lax.ppermute(lax.slice_in_dim(block, block.shape[dim] - width, None, axis...  4.94 us
    gather x2, local copies, waits for them, and re-layouts, couple_add(): picked = piece[jnp.clip(local_idx, 0, rows - 1)]  4.85 us
  transfers between devices with their start and end apart: 3, of which 0 were waited for; matrix products, arithmetic and copies ran while one was open for 14% of the time, Pallas kernels for 0%

commit v1 on v0

v1 whole, which is shorter than its diff:
```python
import functools

import jax
import jax.numpy as jnp
from jax import lax
from jax.experimental import pallas as pl
from jax.experimental.pallas import tpu as pltpu
from jax.sharding import PartitionSpec as P

F32 = jnp.float32
BF16 = jnp.bfloat16
MESH = pl.DeviceIdType.MESH

X, Y, Z = 4, 4, 8
ROWS = 80
HALF = ROWS // 2

U1P, U1M, U2P, U2M = 0, 1, 2, 3
V1P, V1M, V2P, V2M = 4, 8, 12, 16
SIB = 20
COPIES = 36


def mod(a, n):
    return lax.rem(a + n, n)


def stacked(a):
    hi = a.astype(BF16).astype(F32)
    return jnp.concatenate([hi, a - hi], axis=0).astype(BF16)


def split(b):
    hi = b.astype(BF16)
    return hi, (b - hi.astype(F32)).astype(BF16)


def dot(a, b):
    return jnp.dot(a, b, preferred_element_type=F32)


def product2(a, hi, lo):
    both = stacked(a)
    out = dot(both, hi) + dot(both, lo)
    half = out.shape[0] // 2
    return out[:half] + out[half:]


def product(a, b):
    return product2(a, *split(b))


def iota(shape, dim):
    return lax.broadcasted_iota(jnp.int32, shape, dim)


def kernel(
    near_list,
    near_count,
    leaf_count,
    mid_count,
    leaf_list,
    mid_list,
    top_list,
    x_hbm,
    near_hbm,
    leaf_hbm,
    mid_hbm,
    top_hbm,
    lin_hbm,
    lup_hbm,
    mup_hbm,
    mdn_hbm,
    ldn_hbm,
    lout_hbm,
    out_ref,
    xbuf,
    near_v,
    leaf_v,
    mid_v,
    top_v,
    lin_v,
    lup_v,
    mup_v,
    mdn_v,
    ldn_v,
    lout_v,
    coef,
    stage,
    xe,
    near_acc,
    onehot,
    onehot2,
    picked,
    whi,
    wlo,
    w2hi,
    w2lo,
    ohi,
    olo,
    load_sem,
    near_sem,
    halo_send,
    halo_recv,
    z_send,
    z_recv,
    col_send,
    col_recv,
):
    me = lax.axis_index("cluster")
    c = lax.rem(me, 2)
    z = lax.rem(lax.div(me, 2), Z)
    y = lax.rem(lax.div(me, 2 * Z), Y)
    x = lax.div(me, 2 * Z * Y)
    v = x + c * (y - x)
    u = y + c * (x - y)

    def device(vv, uu, zz):
        xx = vv + c * (uu - vv)
        yy = uu + c * (vv - uu)
        return ((xx * Y + yy) * Z + zz) * 2 + c

    sibling = me + 1 - 2 * c
    right = mod(me + 1, 256)
    left = mod(me - 1, 256)

    def load(i, source, target):
        copy = pltpu.make_async_copy(source, target, load_sem.at[i])
        copy.start()
        return copy

    load_x = load(0, x_hbm, xbuf.at[1])
    load_lin = load(1, lin_hbm, lin_v)
    load_lup = load(2, lup_hbm, lup_v)
    load_mup = load(3, mup_hbm, mup_v)
    load_near = []
    for i in range(4):
        copy = pltpu.make_async_copy(
            near_hbm.at[pl.ds(2 * i, 2)], near_v.at[pl.ds(2 * i, 2)], near_sem.at[i]
        )
        copy.start()
        load_near.append(copy)
    load_leaf = load(4, leaf_hbm, leaf_v)
    load_mid = load(5, mid_hbm, mid_v)
    load_top = load(6, top_hbm.at[lax.div(me, 8)], top_v)
    load_mdn = load(7, mdn_hbm, mdn_v)
    load_ldn = load(8, ldn_hbm, ldn_v)
    load_lout = load(9, lout_hbm, lout_v)

    barrier = pltpu.get_barrier_semaphore()
    partners = [device(v, u, mod(z + k, Z)) for k in range(1, Z)]
    up, um = mod(u + 1, 4), mod(u - 1, 4)
    vp, vm = mod(v + 1, 4), mod(v - 1, 4)
    dev_up, dev_um = device(v, up, z), device(v, um, z)
    dev_vp, dev_vm = device(vp, u, z), device(vm, u, z)
    partners += [dev_up, dev_um, dev_vp, dev_vm, sibling, right, left]
    for partner in partners:
        pl.semaphore_signal(barrier, inc=1, device_id=(partner,), device_id_type=MESH)

    load_x.wait()
    load_lin.wait()
    load_lup.wait()
    load_mup.wait()
    zeros64 = jnp.zeros((32, 64), F32)
    r_parts = []
    for i in range(4):
        block = jnp.concatenate(
            [
                jnp.concatenate([lin_v[2 * i], zeros64], axis=1),
                jnp.concatenate([zeros64, lin_v[2 * i + 1]], axis=1),
            ],
            axis=0,
        )
        hi, lo = split(block)
        both = stacked(xbuf[1, :, i * 128 : (i + 1) * 128])
        nt = functools.partial(
            lax.dot_general,
            dimension_numbers=(((1,), (1,)), ((), ())),
            preferred_element_type=F32,
        )
        part = nt(both, hi) + nt(both, lo)
        r_parts.append(part[:8] + part[8:])
    r = jnp.concatenate(r_parts, axis=1)
    lup = lup_v[...].reshape(256, 32)
    both_up = jnp.concatenate([lup, product(lup, mup_v[0])], axis=1)
    p = product(r, both_up)
    rp = jnp.concatenate([r, p, jnp.zeros((8, 64), F32)], axis=1)
    hi = rp.astype(BF16).astype(F32)
    rest = rp - hi
    mid = rest.astype(BF16).astype(F32)
    rp4 = jnp.concatenate([hi, mid, rest - mid, jnp.zeros_like(rp)], axis=0)
    spread = (iota((32, 256), 0) % 8 == iota((32, 256), 1) % 8).astype(BF16)
    rows = dot(jnp.transpose(rp4).astype(BF16), spread)
    rows = rows[:320].reshape(10, 32, 256)
    same = iota((32, 256), 0) == iota((32, 256), 1) // 8
    rows = jnp.sum(jnp.where(same[None], rows, 0.0), axis=1)
    my_rows = pl.ds(pl.multiple_of(z * 8, 8), 8)
    coef[c, v, u, my_rows, :] = rows[:8]
    stage[z] = rows[8:10]

    pl.semaphore_wait(barrier, len(partners))

    def halo(i, source, target, dev):
        return pltpu.make_async_remote_copy(
            src_ref=xbuf.at[source],
            dst_ref=xbuf.at[target],
            send_sem=halo_send.at[i],
            recv_sem=halo_recv.at[i],
            device_id=(dev,),
            device_id_type=MESH,
        )

    def along_z(k, zz, dev):
        return (
            pltpu.make_async_remote_copy(
                src_ref=coef.at[c, v, u, pl.ds(pl.multiple_of(zz * 8, 8), 8)],
                dst_ref=coef.at[c, v, u, pl.ds(pl.multiple_of(zz * 8, 8), 8)],
                send_sem=z_send.at[k, 0],
                recv_sem=z_recv.at[k, 0],
                device_id=(dev,),
                device_id_type=MESH,
            ),
            pltpu.make_async_remote_copy(
                src_ref=stage.at[zz],
                dst_ref=stage.at[zz],
                send_sem=z_send.at[k, 1],
                recv_sem=z_recv.at[k, 1],
                device_id=(dev,),
                device_id_type=MESH,
            ),
        )

    order = [4, 3, 5, 2, 6, 1, 7]
    sends = []
    for k in order:
        pair = along_z(k - 1, z, device(v, u, mod(z + k, Z)))
        for copy in pair:
            copy.start()
        sends += pair
    halo_copies = [halo(0, 1, 0, right), halo(1, 1, 2, left)]
    for copy in halo_copies:
        copy.start()
    sends += halo_copies

    def place(s, shift):
        cc = (s >> shift) & 1
        zz = (s >> (shift + 1)) & 7
        yy = (s >> (shift + 4)) & 3
        xx = (s >> (shift + 6)) & 3
        vv = jnp.where(cc == 0, xx, yy)
        uu = jnp.where(cc == 0, yy, xx)
        return cc * 128 + vv * 32 + uu * 8 + zz

    def live_of(counts, width):
        n = len(counts)
        row = iota((n, width), 0)
        cap = jnp.zeros((n, width), jnp.int32)
        for i, count in enumerate(counts):
            cap = jnp.where(row == i, count, cap)
        return iota((n, width), 1) < cap

    def slots():
        s = leaf_list[...]
        k = place(s, 3) * 8 + (s & 7)
        k = jnp.where(live_of([leaf_count[i] for i in range(8)], 48), k, -1)
        m = mid_list[...]
        km = jnp.where(iota((1, 48), 1) < mid_count[0], place(m, 0), -1)
        pad = jnp.full((16, 80), -1, jnp.int32)
        both = jnp.concatenate([k, jnp.broadcast_to(km, (8, 48))], axis=0)
        cols = jnp.transpose(jnp.concatenate([both, pad], axis=1).astype(F32))
        lanes = iota((48, 256), 1).astype(F32)
        for l in range(8):
            col = jnp.broadcast_to(cols[:48, l : l + 1], (48, 256))
            for q in range(8):
                onehot[l * 48 : (l + 1) * 48, q * 256 : (q + 1) * 256] = jnp.where(
                    lanes + (q * 256.0) == col, 1.0, 0.0
                ).astype(BF16)
        col = jnp.broadcast_to(cols[:48, 8:9], (48, 256))
        onehot2[0:48, :] = jnp.where(lanes == col, 1.0, 0.0).astype(BF16)
        wanted = jnp.where(iota((16, 32), 1) == lax.div(me, 8), top_list[...], 0)
        wanted = jnp.sum(wanted.astype(F32), axis=1, keepdims=True)
        k = iota((16, 256), 1)
        vv, uu = (k >> 5) & 3, (k >> 3) & 3
        xx = jnp.where(k < 128, vv, uu)
        yy = jnp.where(k < 128, uu, vv)
        top = ((xx * 4 + yy) * 2 + ((k & 7) >> 2)).astype(F32)
        onehot2[48:64, :] = jnp.where(
            top == jnp.broadcast_to(wanted, (16, 256)), 1.0, 0.0
        ).astype(BF16)

    slots()

    for k in order:
        zz = mod(z - k, Z)
        for copy in along_z(k - 1, zz, me):
            copy.wait_recv()
    coef[c, v, u, 64:72, :] = stage[:, 0, :]
    coef[c, v, u, 72:80, :] = stage[:, 1, :]

    def column(i, cc, vv, uu, half, dev):
        ref = coef.at[cc, vv, uu]
        if half is not None:
            ref = coef.at[cc, vv, uu, pl.ds(half * HALF, HALF)]
        return pltpu.make_async_remote_copy(
            src_ref=ref,
            dst_ref=ref,
            send_sem=col_send.at[i],
            recv_sem=col_recv.at[i],
            device_id=(dev,),
            device_id_type=MESH,
        )

    def send(i, vv, uu, half, dev):
        copy = column(i, c, vv, uu, half, dev)
        copy.start()
        sends.append(copy)

    def arrive(i, vv, uu, half):
        column(i, c, vv, uu, half, me).wait_recv()

    def second(k, uu):
        send(V1P + k, v, uu, None, dev_vp)
        send(V1M + k, v, uu, None, dev_vm)
        send(SIB + k, v, uu, None, sibling)

    u2, v2 = mod(u + 2, 4), mod(v + 2, 4)
    send(U1P, v, u, None, dev_up)
    send(U1M, v, u, None, dev_um)
    second(0, u)

    for i, (source, target) in enumerate([(1, 0), (1, 2)]):
        halo(i, target, target, me).wait_recv()
    low = iota((8, 128), 1) < 64
    xe[0, 24] = jnp.zeros((8, 128), F32)
    xe[1, 24] = jnp.zeros((8, 128), F32)
    for i in range(12):
        tile = xbuf[i // 4, :, (i % 4) * 128 : (i % 4 + 1) * 128]
        turned = pltpu.roll(tile, 64, 1)
        xe[0, 2 * i] = tile
        xe[1, 2 * i] = turned
        xe[0, 2 * i + 1] = turned
        xe[1, 2 * i + 1] = tile
    base = me * 8 - 8

    def near_pair(i):
        outs = []
        for l in (2 * i, 2 * i + 1):
            count = near_count[l]

            def pick(n, side):
                s = jnp.clip(near_list[l, n] - base, 0, 23)
                return xe[side, jnp.where(n < count, s, 24)]

            parts = [
                jnp.where(low, pick(n, 0), pick(n + 1, 1)) for n in range(0, 26, 2)
            ]
            parts.append(pick(26, 0)[:, :64])
            lhs = jnp.concatenate(parts, axis=1)
            outs.append(product(lhs, near_v[l].reshape(27 * 64, 64)))
        near_acc[:, i * 128 : (i + 1) * 128] = jnp.concatenate(outs, axis=1)

    for i in range(2):
        load_near[i].wait()
        near_pair(i)

    arrive(U1P, v, um, None)
    send(U2P, v, um, 0, dev_up)
    second(3, um)
    arrive(U1M, v, up, None)
    send(U2M, v, up, 1, dev_um)
    second(1, up)

    for i in range(2, 4):
        load_near[i].wait()
        near_pair(i)

    arrive(U2P, v, u2, 0)
    arrive(U2M, v, u2, 1)
    second(2, u2)

    load_leaf.wait()
    load_mid.wait()
    load_top.wait()

    def pack(cp):
        gap = jnp.zeros((32, 16), F32)
        blocks = []
        for l in range(8):
            first, other = (2 * cp, 2 * cp + 1) if l % 2 == 0 else (2 * cp + 1, 2 * cp)
            blocks.append(
                jnp.concatenate([leaf_v[l, first], gap, leaf_v[l, other], gap], axis=1)
            )
        hi, lo = split(jnp.transpose(jnp.concatenate(blocks, axis=0)))
        rows = pl.ds(pl.multiple_of(cp * 128, 128), 128)
        whi[rows, :] = hi
        wlo[rows, :] = lo
        block = jnp.concatenate([mid_v[2 * cp], gap, mid_v[2 * cp + 1], gap], axis=1)
        block = jnp.transpose(
            jnp.concatenate([block, jnp.zeros((96, 128), F32)], axis=0)
        )
        rest = jnp.zeros((48, 32), F32)
        top = jnp.concatenate(
            [top_v[:, 2 * cp + 1, :], rest, top_v[:, 2 * cp, :], rest], axis=0
        )
        top = jnp.concatenate(
            [jnp.zeros((128, 32), F32), top, jnp.zeros((128, 64), F32)], axis=1
        )
        hi, lo = split(block + top)
        w2hi[rows, :] = hi
        w2lo[rows, :] = lo

    lax.fori_loop(0, 8, lambda i, _: (pack(i), 0)[1], 0)

    ks = [(0, u), (3, um), (1, up), (2, u2)]
    for k, uu in ks:
        arrive(V1P + k, vm, uu, None)
        send(V2P + k, vm, uu, 0, dev_vp)
        send(SIB + 4 + k, vm, uu, None, sibling)
        arrive(V1M + k, vp, uu, None)
        send(V2M + k, vp, uu, 1, dev_vm)
        send(SIB + 8 + k, vp, uu, None, sibling)

    lax.fori_loop(8, 16, lambda i, _: (pack(i), 0)[1], 0)

    load_mdn.wait()
    load_ldn.wait()
    load_lout.wait()
    wide = []
    for l in range(8):
        pieces = [lout_v[l]]
        if l:
            pieces.insert(0, jnp.zeros((32, 64 * l), F32))
        if l < 7:
            pieces.append(jnp.zeros((32, 64 * (7 - l)), F32))
        wide.append(jnp.concatenate(pieces, axis=1))
    wide = jnp.concatenate(wide, axis=0)
    down = product(jnp.transpose(ldn_v[...].reshape(256, 32)), wide)
    down2 = product(jnp.transpose(mdn_v[0]), down)
    for rows, value in (
        (pl.ds(0, 256), wide),
        (pl.ds(256, 32), down),
        (pl.ds(288, 32), down2),
        (pl.ds(320, 64), jnp.zeros((64, 512), F32)),
    ):
        hi, lo = split(value)
        ohi[rows, :] = hi
        olo[rows, :] = lo

    def plane(cc, vv, first):
        hi, lo = split(coef[cc, vv, :, 0:64, :].reshape(256, 256))
        lanes = pl.ds(pl.multiple_of((cc * 4 + vv) * 256, 256), 256)
        rows = onehot[:, lanes]
        part = (dot(rows, hi) + dot(rows, lo)).reshape(8, 48, 256)
        if first:
            picked[:, 0:48, :] = part
        else:
            picked[:, 0:48, :] += part

    picked[:, 48:64, :] = jnp.zeros((8, 16, 256), F32)
    plane(c, v, True)
    plane(c, vm, False)
    plane(c, vp, False)

    for k, uu in ks:
        arrive(V2P + k, v2, uu, 0)
        arrive(V2M + k, v2, uu, 1)
        send(SIB + 12 + k, v2, uu, None, sibling)
    plane(c, v2, False)

    for q, vv in enumerate([u, um, up, u2]):
        for k, uu in [(0, v), (3, vm), (1, vp), (2, v2)]:
            column(SIB + 4 * q + k, 1 - c, vv, uu, None, me).wait_recv()
        plane(1 - c, vv, False)

    mid_rows = coef[:, :, :, 64:72, :].reshape(256, 256)
    top_rows = coef[:, :, :, 72:80, :].reshape(256, 256)
    hi, lo = split(mid_rows)
    rows = onehot2[0:48, :]
    mid_picked = dot(rows, hi) + dot(rows, lo)
    hi, lo = split(top_rows)
    rows = onehot2[48:64, :]
    top_picked = dot(rows, hi) + dot(rows, lo)

    turned = [
        jnp.transpose(picked[2 * i : 2 * i + 2].reshape(128, 256)) for i in range(4)
    ]
    gap = jnp.zeros((16, 256), F32)
    turned.append(
        jnp.transpose(
            jnp.concatenate([mid_picked, gap, top_picked, gap, gap, gap], axis=0)
        )
    )
    lhs = []
    for t in turned:
        even, odd = [], []
        for cp in range(16):
            a = t[16 * cp : 16 * cp + 8]
            b = pltpu.roll(t[16 * cp + 8 : 16 * cp + 16], 64, 1)
            even.append(jnp.where(low, a, b))
            odd.append(jnp.where(low, b, a))
        lhs += [jnp.concatenate(even, axis=1), jnp.concatenate(odd, axis=1)]
    far = product2(jnp.concatenate(lhs[:8], axis=0), whi[...], wlo[...])
    far = far.reshape(8, 8, 256)
    own = iota((8, 8, 256), 2) // 32 == iota((8, 8, 256), 0)
    far = jnp.sum(jnp.where(own, far, 0.0), axis=0)
    high = product2(jnp.concatenate(lhs[8:], axis=0), w2hi[...], w2lo[...])
    high = jnp.where(iota((8, 128), 1) < 32, high[:8], high[8:])
    field = jnp.concatenate([far, high], axis=1)
    out_ref[...] = near_acc[...] + product2(field, ohi[...], olo[...])

    for copy in sends:
        copy.wait_send()


def on_device(
    x_block,
    near_tiles,
    near_list,
    near_count,
    leaf_in,
    leaf_up,
    mid_up,
    leaf_tiles,
    leaf_list,
    leaf_count,
    mid_tiles,
    mid_list,
    mid_count,
    top_tiles,
    top_list,
    mid_down,
    leaf_down,
    leaf_out,
):
    smem = pl.BlockSpec(memory_space=pltpu.SMEM)
    vmem = pl.BlockSpec(memory_space=pltpu.VMEM)
    hbm = pl.BlockSpec(memory_space=pl.ANY)
    return pl.pallas_call(
        kernel,
        out_shape=jax.ShapeDtypeStruct((8, 512), F32),
        in_specs=[smem] * 4 + [vmem] * 3 + [hbm] * 11,
        out_specs=vmem,
        scratch_shapes=[
            pltpu.VMEM((3, 8, 512), F32),
            pltpu.VMEM((8, 27, 64, 64), F32),
            pltpu.VMEM((8, 32, 32, 48), F32),
            pltpu.VMEM((32, 32, 48), F32),
            pltpu.VMEM((16, 32, 32), F32),
            pltpu.VMEM((8, 32, 64), F32),
            pltpu.VMEM((8, 32, 32), F32),
            pltpu.VMEM((1, 32, 32), F32),
            pltpu.VMEM((1, 32, 32), F32),
            pltpu.VMEM((8, 32, 32), F32),
            pltpu.VMEM((8, 32, 64), F32),
            pltpu.VMEM((2, 4, 4, ROWS, 256), F32),
            pltpu.VMEM((8, 2, 256), F32),
            pltpu.VMEM((2, 25, 8, 128), F32),
            pltpu.VMEM((8, 512), F32),
            pltpu.VMEM((384, 2048), BF16),
            pltpu.VMEM((64, 256), BF16),
            pltpu.VMEM((8, 64, 256), F32),
            pltpu.VMEM((2048, 256), BF16),
            pltpu.VMEM((2048, 256), BF16),
            pltpu.VMEM((2048, 128), BF16),
            pltpu.VMEM((2048, 128), BF16),
            pltpu.VMEM((384, 512), BF16),
            pltpu.VMEM((384, 512), BF16),
            pltpu.SemaphoreType.DMA((10,)),
            pltpu.SemaphoreType.DMA((4,)),
            pltpu.SemaphoreType.DMA((2,)),
            pltpu.SemaphoreType.DMA((2,)),
            pltpu.SemaphoreType.DMA((7, 2)),
            pltpu.SemaphoreType.DMA((7, 2)),
            pltpu.SemaphoreType.DMA((COPIES,)),
            pltpu.SemaphoreType.DMA((COPIES,)),
        ],
        compiler_params=pltpu.CompilerParams(
            collective_id=0, has_side_effects=True, vmem_limit_bytes=50 * 2**20
        ),
    )(
        near_list,
        near_count,
        leaf_count,
        mid_count,
        leaf_list,
        mid_list,
        top_list.T,
        x_block,
        near_tiles,
        leaf_tiles.transpose(0, 2, 3, 1),
        mid_tiles[0].transpose(1, 2, 0),
        top_tiles,
        leaf_in.transpose(0, 2, 1),
        leaf_up,
        mid_up,
        mid_down,
        leaf_down,
        leaf_out.transpose(0, 2, 1),
    )


def solution(mesh):
    placed = (
        P(None, "cluster"),
        P("cluster", None, None, None),
        P("cluster", None),
        P("cluster"),
        P("cluster", None, None),
        P("cluster", None, None),
        P("cluster", None, None),
        P("cluster", None, None, None),
        P("cluster", None),
        P("cluster"),
        P("cluster", None, None, None),
        P("cluster", None),
        P("cluster"),
        P(),
        P(),
        P("cluster", None, None),
        P("cluster", None, None),
        P("cluster", None, None),
    )
    return jax.shard_map(
        on_device, mesh=mesh, in_specs=placed, out_specs=P(None, "cluster"), check_vma=False
    )
```

time: 194 us -> 47.6 us (0.25)
  blocking collectives: 128 us -> 0 us
  Pallas kernels: 0 us -> 35 us
  matrix products: 23.8 us -> 0 us
  between operations: 14.3 us -> 0.68 us
  local copies, waits for them, and re-layouts: 18.5 us -> 11.4 us
  starting transfers between devices: 6.9 us -> 0 us
  other arithmetic: 2.34 us -> 0 us
    all_gather x2 -> x0, blocking collectives: 128 us -> none  [the longest x1 67.3 us: on_device(): shares = lax.all_gather(share[None], 'cluster', axis=0, tiled=True)]
    pallas_call x0 -> x1, Pallas kernels: none -> 35 us  [on_device(): pl.pallas_call(kernel, out_shape=jax.ShapeDtypeStruct((8, 512), F32), in_...]
    dot_general x10 -> x0, matrix products: 23.8 us -> none  [the longest x2 11.5 us: couple_add(): jnp.einsum('ljca,ljcr,lj->lar', tiles, picked, inside.astype(jnp.float32)...]
    ppermute x2 -> x0, starting transfers between devices: 6.86 us -> none  [the longest x1 4.94 us: with_halo(): lax.ppermute(lax.slice_in_dim(block, block.shape[dim] - width, None, axis...]
    gather x4 -> x0, local copies, waits for them, and re-layouts: 6.36 us -> none  [the longest x2 4.85 us: couple_add(): picked = piece[jnp.clip(local_idx, 0, rows - 1)]]
    unnamed x17 -> x29, local copies, waits for them, and re-layouts: 7.73 us -> 11.4 us
  transfers between devices with their start and end apart: 3 -> 0, of which waited for: 0 -> 0; matrix products, arithmetic and copies ran while one was open for 14% -> 0% of each run, Pallas kernels for 0% -> 0%
where the time goes in v1:
time: 47.6 us; the launch traced here: 47.1 us
  Pallas kernels  35 us (74%)
  local copies, waits for them, and re-layouts  11.4 us (24%)
  between operations  0.68 us (1%)
    pallas_call x1, Pallas kernels, on_device(): pl.pallas_call(kernel, out_shape=jax.ShapeDtypeStruct((8, 512), F32), in_...  35 us
    unnamed x29, local copies, waits for them, and re-layouts  11.4 us

profile of v1, /device:TPU:1, one launch (start us, length us, event | category | flops | bytes accessed | tf_op | source)
XLA Modules:
  0.0 47.1 jit_solution(16382048255465338302)
XLA Ops:
  0.7 0.0 copy-start
  0.7 1.0 %copy-done = f32[1,48,32,32]{1,3,2,0:T(8,128)S(1)} copy-done((f32[1,48,32,32]{1,3,2,0:T(8,128)S(1)}, f32[1,48,32,32]{1,3,2,0:T(8,128)}, u32[]{:S(2)}) %copy-start) | copy-done | bytes 196632
  1.7 0.0 copy-start.1
  1.7 0.9 %copy-done.1 = f32[8,64,32]{1,2,0:T(8,128)S(1)} copy-done((f32[8,64,32]{1,2,0:T(8,128)S(1)}, f32[8,64,32]{1,2,0:T(8,128)}, u32[]{:S(2)}) %copy-start.1) | copy-done | bytes 65560
  2.6 0.0 copy-start.2
  2.6 0.9 %copy-done.2 = f32[8,32,32]{2,1,0:T(8,128)S(1)} copy-done((f32[8,32,32]{2,1,0:T(8,128)S(1)}, f32[8,32,32]{2,1,0:T(8,128)}, u32[]{:S(2)}) %copy-start.2) | copy-done | bytes 32792
  3.5 0.0 copy-start.3
  3.5 0.9 %copy-done.3 = f32[8,32,32]{2,1,0:T(8,128)S(1)} copy-done((f32[8,32,32]{2,1,0:T(8,128)S(1)}, f32[8,32,32]{2,1,0:T(8,128)}, u32[]{:S(2)}) %copy-start.3) | copy-done | bytes 32792
  4.4 0.0 copy-start.4
  4.4 0.9 %copy-done.4 = f32[8,64,32]{1,2,0:T(8,128)S(1)} copy-done((f32[8,64,32]{1,2,0:T(8,128)S(1)}, f32[8,64,32]{1,2,0:T(8,128)}, u32[]{:S(2)}) %copy-start.4) | copy-done | bytes 65560
  5.3 0.0 copy-start.5
  5.3 0.7 %copy-done.5 = f32[8,512]{1,0:T(8,128)S(1)} copy-done((f32[8,512]{1,0:T(8,128)S(1)}, f32[8,512]{1,0:T(8,128)}, u32[]{:S(2)}) %copy-start.5) | copy-done | bytes 16408
  6.0 0.0 copy-start.6
  6.0 0.7 %copy-done.6 = f32[1,32,32]{2,1,0:T(8,128)S(1)} copy-done((f32[1,32,32]{2,1,0:T(8,128)S(1)}, f32[1,32,32]{2,1,0:T(8,128)}, u32[]{:S(2)}) %copy-start.6) | copy-done | bytes 4120
  6.8 0.0 copy-start.7
  6.8 0.7 %copy-done.7 = f32[1,32,32]{2,1,0:T(8,128)S(1)} copy-done((f32[1,32,32]{2,1,0:T(8,128)S(1)}, f32[1,32,32]{2,1,0:T(8,128)}, u32[]{:S(2)}) %copy-start.7) | copy-done | bytes 4120
  7.5 0.0 copy-start.8
  7.5 0.7 %copy-done.8 = s32[32,16]{0,1:T(8,128)S(1)} copy-done((s32[32,16]{0,1:T(8,128)S(1)}, s32[32,16]{0,1:T(8,128)}, u32[]{:S(2)}) %copy-start.8) | copy-done | bytes 2072
  8.2 0.0 copy-start.9
  8.2 0.7 %copy-done.9 = s32[8,27]{1,0:T(8,128)S(1)} copy-done((s32[8,27]{1,0:T(8,128)S(1)}, s32[8,27]{1,0:T(8,128)}, u32[]{:S(2)}) %copy-start.9) | copy-done | bytes 888
  8.9 0.0 copy-start.10
  8.9 0.7 %copy-done.10 = s32[8,48]{1,0:T(8,128)S(1)} copy-done((s32[8,48]{1,0:T(8,128)S(1)}, s32[8,48]{1,0:T(8,128)}, u32[]{:S(2)}) %copy-start.10) | copy-done | bytes 1560
  9.5 0.0 copy-start.11
  9.5 0.7 %copy-done.11 = s32[8]{0:T(128)S(1)} copy-done((s32[8]{0:T(128)S(1)}, s32[8]{0:T(128)}, u32[]{:S(2)}) %copy-start.11) | copy-done | bytes 56
  10.2 0.0 copy-start.12
  10.2 0.7 %copy-done.12 = s32[8]{0:T(128)S(1)} copy-done((s32[8]{0:T(128)S(1)}, s32[8]{0:T(128)}, u32[]{:S(2)}) %copy-start.12) | copy-done | bytes 56
  10.9 0.0 copy-start.13
  10.9 0.7 %copy-done.13 = s32[1,48]{1,0:T(1,128)S(1)} copy-done((s32[1,48]{1,0:T(1,128)S(1)}, s32[1,48]{1,0:T(1,128)}, u32[]{:S(2)}) %copy-start.13) | copy-done | bytes 216
  11.5 35.0 %shard_map.172 = f32[8,512]{1,0:T(8,128)S(1)} custom-call(s32[8,27]{1,0:T(8,128)S(1)} %copy-done.9, s32[8]{0:T(128)S(1)} %copy-done.11, s32[8]{0:T(128)S(1)} %copy-done.12, s32[1]{0:T(128)S(6)} %copy.20.mid_count, s32[8,48]{1,0:T(8,128)S(1)} %copy-done.10, s32[1,48]{1,0:T(1,128)S(1)} %copy-done.13, s32[16,32]{1,0:T(8,128)S(1)} %bitcast.10, ...), custom_call_target="tpu_custom_call" | custom-call | tf_op jit(solution)/shard_map/pallas_call | solution.py:538
  46.5 0.6 %copy.21 = f32[8,512]{1,0:T(8,128)} copy(f32[8,512]{1,0:T(8,128)S(1)} %shard_map.172) | data formatting | bytes 32768
Async XLA Ops:
  0.7 1.0 %copy-start = (f32[1,48,32,32]{1,3,2,0:T(8,128)S(1)}, f32[1,48,32,32]{1,3,2,0:T(8,128)}, u32[]{:S(2)}) copy-start(f32[1,48,32,32]{1,3,2,0:T(8,128)} %param.28) | copy-start | bytes 589828
  1.7 0.9 %copy-start.1 = (f32[8,64,32]{1,2,0:T(8,128)S(1)}, f32[8,64,32]{1,2,0:T(8,128)}, u32[]{:S(2)}) copy-start(f32[8,64,32]{1,2,0:T(8,128)} %param.22) | copy-start | bytes 196612
  2.6 0.9 %copy-start.2 = (f32[8,32,32]{2,1,0:T(8,128)S(1)}, f32[8,32,32]{2,1,0:T(8,128)}, u32[]{:S(2)}) copy-start(f32[8,32,32]{2,1,0:T(8,128)} %lup_hbm.1) | copy-start | bytes 98308
  3.5 0.9 %copy-start.3 = (f32[8,32,32]{2,1,0:T(8,128)S(1)}, f32[8,32,32]{2,1,0:T(8,128)}, u32[]{:S(2)}) copy-start(f32[8,32,32]{2,1,0:T(8,128)} %ldn_hbm.1) | copy-start | bytes 98308
  4.4 0.9 %copy-start.4 = (f32[8,64,32]{1,2,0:T(8,128)S(1)}, f32[8,64,32]{1,2,0:T(8,128)}, u32[]{:S(2)}) copy-start(f32[8,64,32]{1,2,0:T(8,128)} %param.35) | copy-start | bytes 196612
  5.3 0.7 %copy-start.5 = (f32[8,512]{1,0:T(8,128)S(1)}, f32[8,512]{1,0:T(8,128)}, u32[]{:S(2)}) copy-start(f32[8,512]{1,0:T(8,128)} %x_hbm.1) | copy-start | bytes 49156
  6.0 0.7 %copy-start.6 = (f32[1,32,32]{2,1,0:T(8,128)S(1)}, f32[1,32,32]{2,1,0:T(8,128)}, u32[]{:S(2)}) copy-start(f32[1,32,32]{2,1,0:T(8,128)} %mup_hbm.1) | copy-start | bytes 12292
  6.8 0.7 %copy-start.7 = (f32[1,32,32]{2,1,0:T(8,128)S(1)}, f32[1,32,32]{2,1,0:T(8,128)}, u32[]{:S(2)}) copy-start(f32[1,32,32]{2,1,0:T(8,128)} %mdn_hbm.1) | copy-start | bytes 12292
  7.5 0.7 %copy-start.8 = (s32[32,16]{0,1:T(8,128)S(1)}, s32[32,16]{0,1:T(8,128)}, u32[]{:S(2)}) copy-start(s32[32,16]{0,1:T(8,128)} %param.32) | copy-start | bytes 6148
  8.2 0.7 %copy-start.9 = (s32[8,27]{1,0:T(8,128)S(1)}, s32[8,27]{1,0:T(8,128)}, u32[]{:S(2)}) copy-start(s32[8,27]{1,0:T(8,128)} %near_list.1) | copy-start | bytes 2596
  8.9 0.7 %copy-start.10 = (s32[8,48]{1,0:T(8,128)S(1)}, s32[8,48]{1,0:T(8,128)}, u32[]{:S(2)}) copy-start(s32[8,48]{1,0:T(8,128)} %leaf_list.1) | copy-start | bytes 4612
  9.5 0.7 %copy-start.11 = (s32[8]{0:T(128)S(1)}, s32[8]{0:T(128)}, u32[]{:S(2)}) copy-start(s32[8]{0:T(128)} %near_count.1) | copy-start | bytes 100
  10.2 0.7 %copy-start.12 = (s32[8]{0:T(128)S(1)}, s32[8]{0:T(128)}, u32[]{:S(2)}) copy-start(s32[8]{0:T(128)} %leaf_count.1) | copy-start | bytes 100
  10.9 0.7 %copy-start.13 = (s32[1,48]{1,0:T(1,128)S(1)}, s32[1,48]{1,0:T(1,128)}, u32[]{:S(2)}) copy-start(s32[1,48]{1,0:T(1,128)} %mid_list.1) | copy-start | bytes 580

commit v2 on v1

--- a/solution.py
+++ b/solution.py
@@ -13,12 +13,11 @@
 
 X, Y, Z = 4, 4, 8
 ROWS = 80
+
 HALF = ROWS // 2
-
-U1P, U1M, U2P, U2M = 0, 1, 2, 3
-V1P, V1M, V2P, V2M = 4, 8, 12, 16
-SIB = 20
-COPIES = 36
+U_ID, V_ID, W_ID = 0, 3, 15
+FORWARDED = 3
+COPIES = 24
 
 
 def mod(a, n):
@@ -55,13 +54,13 @@
 
 
 def kernel(
-    near_list,
-    near_count,
-    leaf_count,
-    mid_count,
-    leaf_list,
-    mid_list,
-    top_list,
+    near_list_hbm,
+    near_count_hbm,
+    leaf_count_hbm,
+    mid_count_hbm,
+    leaf_list_hbm,
+    mid_list_hbm,
+    top_list_hbm,
     x_hbm,
     near_hbm,
     leaf_hbm,
@@ -74,6 +73,13 @@
     ldn_hbm,
     lout_hbm,
     out_ref,
+    near_list,
+    near_count,
+    leaf_count,
+    mid_count,
+    leaf_list,
+    mid_list,
+    top_list,
     xbuf,
     near_v,
     leaf_v,
@@ -106,6 +112,9 @@
     z_recv,
     col_send,
     col_recv,
+    wanted_rows,
+    swap_send,
+    swap_recv,
 ):
     me = lax.axis_index("cluster")
     c = lax.rem(me, 2)
@@ -133,27 +142,15 @@
     load_lin = load(1, lin_hbm, lin_v)
     load_lup = load(2, lup_hbm, lup_v)
     load_mup = load(3, mup_hbm, mup_v)
-    load_near = []
-    for i in range(4):
-        copy = pltpu.make_async_copy(
-            near_hbm.at[pl.ds(2 * i, 2)], near_v.at[pl.ds(2 * i, 2)], near_sem.at[i]
-        )
-        copy.start()
-        load_near.append(copy)
-    load_leaf = load(4, leaf_hbm, leaf_v)
-    load_mid = load(5, mid_hbm, mid_v)
-    load_top = load(6, top_hbm.at[lax.div(me, 8)], top_v)
-    load_mdn = load(7, mdn_hbm, mdn_v)
-    load_ldn = load(8, ldn_hbm, ldn_v)
-    load_lout = load(9, lout_hbm, lout_v)
-
     barrier = pltpu.get_barrier_semaphore()
     partners = [device(v, u, mod(z + k, Z)) for k in range(1, Z)]
     up, um = mod(u + 1, 4), mod(u - 1, 4)
     vp, vm = mod(v + 1, 4), mod(v - 1, 4)
     dev_up, dev_um = device(v, up, z), device(v, um, z)
     dev_vp, dev_vm = device(vp, u, z), device(vm, u, z)
-    partners += [dev_up, dev_um, dev_vp, dev_vm, sibling, right, left]
+    u2, v2 = mod(u + 2, 4), mod(v + 2, 4)
+    dev_u2, dev_v2 = device(v, u2, z), device(v2, u, z)
+    partners += [dev_up, dev_um, dev_u2, dev_vp, dev_vm, dev_v2, sibling, right, left]
     for partner in partners:
         pl.semaphore_signal(barrier, inc=1, device_id=(partner,), device_id_type=MESH)
 
@@ -183,20 +180,22 @@
     r = jnp.concatenate(r_parts, axis=1)
     lup = lup_v[...].reshape(256, 32)
     both_up = jnp.concatenate([lup, product(lup, mup_v[0])], axis=1)
-    p = product(r, both_up)
-    rp = jnp.concatenate([r, p, jnp.zeros((8, 64), F32)], axis=1)
-    hi = rp.astype(BF16).astype(F32)
-    rest = rp - hi
-    mid = rest.astype(BF16).astype(F32)
-    rp4 = jnp.concatenate([hi, mid, rest - mid, jnp.zeros_like(rp)], axis=0)
     spread = (iota((32, 256), 0) % 8 == iota((32, 256), 1) % 8).astype(BF16)
-    rows = dot(jnp.transpose(rp4).astype(BF16), spread)
-    rows = rows[:320].reshape(10, 32, 256)
     same = iota((32, 256), 0) == iota((32, 256), 1) // 8
-    rows = jnp.sum(jnp.where(same[None], rows, 0.0), axis=1)
+
+    def flat(a):
+        n = a.shape[1] // 32
+        if n % 4:
+            a = jnp.concatenate([a, jnp.zeros((8, 32 * (4 - n % 4)), F32)], axis=1)
+        hi = a.astype(BF16).astype(F32)
+        rest = a - hi
+        mid = rest.astype(BF16).astype(F32)
+        parts = jnp.concatenate([hi, mid, rest - mid, jnp.zeros_like(a)], axis=0)
+        rows = dot(jnp.transpose(parts).astype(BF16), spread)[: 32 * n]
+        return jnp.sum(jnp.where(same[None], rows.reshape(n, 32, 256), 0.0), axis=1)
+
     my_rows = pl.ds(pl.multiple_of(z * 8, 8), 8)
-    coef[c, v, u, my_rows, :] = rows[:8]
-    stage[z] = rows[8:10]
+    coef[c, v, u, my_rows, :] = flat(r)
 
     pl.semaphore_wait(barrier, len(partners))
 
@@ -233,10 +232,37 @@
     order = [4, 3, 5, 2, 6, 1, 7]
     sends = []
     for k in order:
-        pair = along_z(k - 1, z, device(v, u, mod(z + k, Z)))
-        for copy in pair:
-            copy.start()
-        sends += pair
+        copy = along_z(k - 1, z, device(v, u, mod(z + k, Z)))[0]
+        copy.start()
+        sends.append(copy)
+    stage[z] = flat(product(r, both_up))
+    for k in order:
+        copy = along_z(k - 1, z, device(v, u, mod(z + k, Z)))[1]
+        copy.start()
+        sends.append(copy)
+    load_lists = [
+        load(10, leaf_count_hbm, leaf_count),
+        load(11, mid_count_hbm, mid_count),
+        load(12, leaf_list_hbm, leaf_list),
+        load(13, mid_list_hbm, mid_list),
+        load(14, top_list_hbm, top_list),
+        load(15, near_list_hbm, near_list),
+        load(16, near_count_hbm, near_count),
+    ]
+    load_near = []
+    for i in range(4):
+        copy = pltpu.make_async_copy(
+            near_hbm.at[pl.ds(2 * i, 2)], near_v.at[pl.ds(2 * i, 2)], near_sem.at[i]
+        )
+        copy.start()
+        load_near.append(copy)
+    load_leaf = load(4, leaf_hbm, leaf_v)
+    load_mid = load(5, mid_hbm, mid_v)
+    load_top = load(6, top_hbm.at[lax.div(me, 8)], top_v)
+    load_mdn = load(7, mdn_hbm, mdn_v)
+    load_ldn = load(8, ldn_hbm, ldn_v)
+    load_lout = load(9, lout_hbm, lout_v)
+
     halo_copies = [halo(0, 1, 0, right), halo(1, 1, 2, left)]
     for copy in halo_copies:
         copy.start()
@@ -249,7 +275,7 @@
         xx = (s >> (shift + 6)) & 3
         vv = jnp.where(cc == 0, xx, yy)
         uu = jnp.where(cc == 0, yy, xx)
-        return cc * 128 + vv * 32 + uu * 8 + zz
+        return cc, uu * 32 + vv * 8 + zz
 
     def live_of(counts, width):
         n = len(counts)
@@ -261,34 +287,59 @@
 
     def slots():
         s = leaf_list[...]
-        k = place(s, 3) * 8 + (s & 7)
+        cc, k = place(s, 3)
+        k = cc * 1024 + k * 8 + (s & 7)
         k = jnp.where(live_of([leaf_count[i] for i in range(8)], 48), k, -1)
-        m = mid_list[...]
-        km = jnp.where(iota((1, 48), 1) < mid_count[0], place(m, 0), -1)
+        cc, km = place(mid_list[...], 0)
+        km = cc * 256 + (km >> 3) * 16 + (km & 7)
+        km = jnp.where(iota((1, 48), 1) < mid_count[0, 0], km, -1)
+        both = jnp.concatenate([k, jnp.broadcast_to(km, (8, 48))], axis=0)
         pad = jnp.full((16, 80), -1, jnp.int32)
-        both = jnp.concatenate([k, jnp.broadcast_to(km, (8, 48))], axis=0)
-        cols = jnp.transpose(jnp.concatenate([both, pad], axis=1).astype(F32))
+        wanted_rows[0] = jnp.concatenate([both, pad], axis=1).astype(F32)
+
+    def list_copy():
+        return pltpu.make_async_remote_copy(
+            src_ref=wanted_rows.at[0],
+            dst_ref=wanted_rows.at[1],
+            send_sem=swap_send.at[0],
+            recv_sem=swap_recv.at[0],
+            device_id=(sibling,),
+            device_id_type=MESH,
+        )
+
+    def one_hot(side):
+        cols = jnp.transpose(wanted_rows[side])
+        start = (c * 1024).astype(F32)
         lanes = iota((48, 256), 1).astype(F32)
         for l in range(8):
-            col = jnp.broadcast_to(cols[:48, l : l + 1], (48, 256))
-            for q in range(8):
-                onehot[l * 48 : (l + 1) * 48, q * 256 : (q + 1) * 256] = jnp.where(
-                    lanes + (q * 256.0) == col, 1.0, 0.0
+            col = jnp.broadcast_to(cols[:48, l : l + 1], (48, 256)) - start
+            rows = slice(side * 384 + l * 48, side * 384 + (l + 1) * 48)
+            for t in range(4):
+                onehot[rows, t * 256 : (t + 1) * 256] = jnp.where(
+                    lanes + (t * 256.0) == col, 1.0, 0.0
                 ).astype(BF16)
-        col = jnp.broadcast_to(cols[:48, 8:9], (48, 256))
-        onehot2[0:48, :] = jnp.where(lanes == col, 1.0, 0.0).astype(BF16)
+        start = (c * 256).astype(F32)
+        col = jnp.broadcast_to(cols[:48, 8:9], (48, 256)) - start
+        onehot2[side * 64 : side * 64 + 48, :] = jnp.where(
+            lanes == col, 1.0, 0.0
+        ).astype(BF16)
         wanted = jnp.where(iota((16, 32), 1) == lax.div(me, 8), top_list[...], 0)
         wanted = jnp.sum(wanted.astype(F32), axis=1, keepdims=True)
         k = iota((16, 256), 1)
-        vv, uu = (k >> 5) & 3, (k >> 3) & 3
-        xx = jnp.where(k < 128, vv, uu)
-        yy = jnp.where(k < 128, uu, vv)
-        top = ((xx * 4 + yy) * 2 + ((k & 7) >> 2)).astype(F32)
-        onehot2[48:64, :] = jnp.where(
+        uu, vv = (k >> 6) & 3, (k >> 4) & 3
+        xx = vv + c * (uu - vv)
+        yy = uu + c * (vv - uu)
+        top = (xx * 4 + yy) * 2 + ((k & 7) >> 2)
+        top = jnp.where((k & 8) == 8, top, -1).astype(F32)
+        onehot2[side * 64 + 48 : side * 64 + 64, :] = jnp.where(
             top == jnp.broadcast_to(wanted, (16, 256)), 1.0, 0.0
         ).astype(BF16)
 
+    for copy in load_lists:
+        copy.wait()
     slots()
+    list_copy().start()
+    one_hot(0)
 
     for k in order:
         zz = mod(z - k, Z)
@@ -297,10 +348,10 @@
     coef[c, v, u, 64:72, :] = stage[:, 0, :]
     coef[c, v, u, 72:80, :] = stage[:, 1, :]
 
-    def column(i, cc, vv, uu, half, dev):
-        ref = coef.at[cc, vv, uu]
+    def column(i, vv, uu, dev, half=None):
+        ref = coef.at[c, vv, uu]
         if half is not None:
-            ref = coef.at[cc, vv, uu, pl.ds(half * HALF, HALF)]
+            ref = coef.at[c, vv, uu, pl.ds(half * HALF, HALF)]
         return pltpu.make_async_remote_copy(
             src_ref=ref,
             dst_ref=ref,
@@ -310,23 +361,23 @@
             device_id_type=MESH,
         )
 
-    def send(i, vv, uu, half, dev):
-        copy = column(i, c, vv, uu, half, dev)
+    def send(i, vv, uu, dev, half=None):
+        copy = column(i, vv, uu, dev, half)
         copy.start()
         sends.append(copy)
 
-    def arrive(i, vv, uu, half):
-        column(i, c, vv, uu, half, me).wait_recv()
-
-    def second(k, uu):
-        send(V1P + k, v, uu, None, dev_vp)
-        send(V1M + k, v, uu, None, dev_vm)
-        send(SIB + k, v, uu, None, sibling)
-
-    u2, v2 = mod(u + 2, 4), mod(v + 2, 4)
-    send(U1P, v, u, None, dev_up)
-    send(U1M, v, u, None, dev_um)
-    second(0, u)
+    def along_v(k, uu):
+        if k >= FORWARDED:
+            send(V_ID + 3 * k, v, uu, dev_v2)
+        send(V_ID + 3 * k + 1, v, uu, dev_vp)
+        send(V_ID + 3 * k + 2, v, uu, dev_vm)
+
+    send(U_ID, v, u, dev_u2)
+    send(U_ID + 1, v, u, dev_up)
+    send(U_ID + 2, v, u, dev_um)
+    along_v(0, u)
+    list_copy().wait_recv()
+    one_hot(1)
 
     for i, (source, target) in enumerate([(1, 0), (1, 2)]):
         halo(i, target, target, me).wait_recv()
@@ -359,24 +410,16 @@
             outs.append(product(lhs, near_v[l].reshape(27 * 64, 64)))
         near_acc[:, i * 128 : (i + 1) * 128] = jnp.concatenate(outs, axis=1)
 
-    for i in range(2):
+    for i in range(4):
         load_near[i].wait()
         near_pair(i)
 
-    arrive(U1P, v, um, None)
-    send(U2P, v, um, 0, dev_up)
-    second(3, um)
-    arrive(U1M, v, up, None)
-    send(U2M, v, up, 1, dev_um)
-    second(1, up)
-
-    for i in range(2, 4):
-        load_near[i].wait()
-        near_pair(i)
-
-    arrive(U2P, v, u2, 0)
-    arrive(U2M, v, u2, 1)
-    second(2, u2)
+    column(U_ID + 1, v, um, me).wait_recv()
+    along_v(1, um)
+    column(U_ID + 2, v, up, me).wait_recv()
+    along_v(2, up)
+    column(U_ID, v, u2, me).wait_recv()
+    along_v(3, u2)
 
     load_leaf.wait()
     load_mid.wait()
@@ -409,18 +452,7 @@
         w2hi[rows, :] = hi
         w2lo[rows, :] = lo
 
-    lax.fori_loop(0, 8, lambda i, _: (pack(i), 0)[1], 0)
-
-    ks = [(0, u), (3, um), (1, up), (2, u2)]
-    for k, uu in ks:
-        arrive(V1P + k, vm, uu, None)
-        send(V2P + k, vm, uu, 0, dev_vp)
-        send(SIB + 4 + k, vm, uu, None, sibling)
-        arrive(V1M + k, vp, uu, None)
-        send(V2M + k, vp, uu, 1, dev_vm)
-        send(SIB + 8 + k, vp, uu, None, sibling)
-
-    lax.fori_loop(8, 16, lambda i, _: (pack(i), 0)[1], 0)
+    lax.fori_loop(0, 16, lambda i, _: (pack(i), 0)[1], 0)
 
     load_mdn.wait()
     load_ldn.wait()
@@ -446,50 +478,62 @@
         ohi[rows, :] = hi
         olo[rows, :] = lo
 
-    def plane(cc, vv, first):
-        hi, lo = split(coef[cc, vv, :, 0:64, :].reshape(256, 256))
-        lanes = pl.ds(pl.multiple_of((cc * 4 + vv) * 256, 256), 256)
-        rows = onehot[:, lanes]
-        part = (dot(rows, hi) + dot(rows, lo)).reshape(8, 48, 256)
+    def plane(uu, side, first):
+        hi, lo = split(coef[c, :, uu, 0:64, :].reshape(256, 256))
+        lanes = pl.ds(pl.multiple_of(uu * 256, 256), 256)
+        rows = onehot[side * 384 : (side + 1) * 384, lanes]
+        part = dot(rows, hi) + dot(rows, lo)
         if first:
-            picked[:, 0:48, :] = part
+            picked[side, 0:384, :] = part
         else:
-            picked[:, 0:48, :] += part
-
-    picked[:, 48:64, :] = jnp.zeros((8, 16, 256), F32)
-    plane(c, v, True)
-    plane(c, vm, False)
-    plane(c, vp, False)
-
-    for k, uu in ks:
-        arrive(V2P + k, v2, uu, 0)
-        arrive(V2M + k, v2, uu, 1)
-        send(SIB + 12 + k, v2, uu, None, sibling)
-    plane(c, v2, False)
-
-    for q, vv in enumerate([u, um, up, u2]):
-        for k, uu in [(0, v), (3, vm), (1, vp), (2, v2)]:
-            column(SIB + 4 * q + k, 1 - c, vv, uu, None, me).wait_recv()
-        plane(1 - c, vv, False)
-
-    mid_rows = coef[:, :, :, 64:72, :].reshape(256, 256)
-    top_rows = coef[:, :, :, 72:80, :].reshape(256, 256)
-    hi, lo = split(mid_rows)
-    rows = onehot2[0:48, :]
-    mid_picked = dot(rows, hi) + dot(rows, lo)
-    hi, lo = split(top_rows)
-    rows = onehot2[48:64, :]
-    top_picked = dot(rows, hi) + dot(rows, lo)
-
-    turned = [
-        jnp.transpose(picked[2 * i : 2 * i + 2].reshape(128, 256)) for i in range(4)
-    ]
+            picked[side, 0:384, :] += part
+
+    def upper(side):
+        hi, lo = split(coef[c, :, :, 64:80, :].swapaxes(0, 1).reshape(256, 256))
+        rows = onehot2[side * 64 : (side + 1) * 64, :]
+        picked[side, 384:448, :] = dot(rows, hi) + dot(rows, lo)
+
+    def swap():
+        return pltpu.make_async_remote_copy(
+            src_ref=picked.at[1],
+            dst_ref=picked.at[2],
+            send_sem=swap_send.at[1],
+            recv_sem=swap_recv.at[1],
+            device_id=(sibling,),
+            device_id_type=MESH,
+        )
+
+    for k, uu in enumerate([u, um, up, u2]):
+        column(V_ID + 3 * k + 1, vm, uu, me).wait_recv()
+        if k < FORWARDED:
+            send(W_ID + 2 * k, vm, uu, dev_vp, 0)
+        column(V_ID + 3 * k + 2, vp, uu, me).wait_recv()
+        if k < FORWARDED:
+            send(W_ID + 2 * k + 1, vp, uu, dev_vm, 1)
+    for k, uu in enumerate([u, um, up, u2]):
+        if k < FORWARDED:
+            column(W_ID + 2 * k, v2, uu, me, 0).wait_recv()
+            column(W_ID + 2 * k + 1, v2, uu, me, 1).wait_recv()
+        else:
+            column(V_ID + 3 * k, v2, uu, me).wait_recv()
+        if k < 3:
+            plane(uu, 1, k == 0)
+            plane(uu, 0, k == 0)
+    upper(1)
+    plane(u2, 1, False)
+    swap().start()
+    upper(0)
+    plane(u2, 0, False)
+    swap().wait_recv()
+    total = picked[0] + picked[2]
+
     gap = jnp.zeros((16, 256), F32)
-    turned.append(
-        jnp.transpose(
-            jnp.concatenate([mid_picked, gap, top_picked, gap, gap, gap], axis=0)
-        )
-    )
+    turned = []
+    for i in range(5):
+        first, second = total[96 * i : 96 * i + 48], total[96 * i + 48 : 96 * i + 96]
+        if i == 4:
+            second = jnp.concatenate([second, gap, gap], axis=0)
+        turned.append(jnp.transpose(jnp.concatenate([first, gap, second, gap], axis=0)))
     lhs = []
     for t in turned:
         even, odd = [], []
@@ -508,7 +552,7 @@
     field = jnp.concatenate([far, high], axis=1)
     out_ref[...] = near_acc[...] + product2(field, ohi[...], olo[...])
 
-    for copy in sends:
+    for copy in sends + [list_copy(), swap()]:
         copy.wait_send()
 
 
@@ -532,15 +576,21 @@
     leaf_down,
     leaf_out,
 ):
-    smem = pl.BlockSpec(memory_space=pltpu.SMEM)
     vmem = pl.BlockSpec(memory_space=pltpu.VMEM)
-    hbm = pl.BlockSpec(memory_space=pl.ANY)
+    hbm = pl.BlockSpec(memory_space=pltpu.HBM)
     return pl.pallas_call(
         kernel,
-        out_shape=jax.ShapeDtypeStruct((8, 512), F32),
-        in_specs=[smem] * 4 + [vmem] * 3 + [hbm] * 11,
+        out_shape=pltpu.VMEM((8, 512), F32),
+        in_specs=[hbm] * 18,
         out_specs=vmem,
         scratch_shapes=[
+            pltpu.SMEM((8, 27), jnp.int32),
+            pltpu.SMEM((8,), jnp.int32),
+            pltpu.SMEM((8,), jnp.int32),
+            pltpu.SMEM((1, 1), jnp.int32),
+            pltpu.VMEM((8, 48), jnp.int32),
+            pltpu.VMEM((1, 48), jnp.int32),
+            pltpu.VMEM((16, 32), jnp.int32),
             pltpu.VMEM((3, 8, 512), F32),
             pltpu.VMEM((8, 27, 64, 64), F32),
             pltpu.VMEM((8, 32, 32, 48), F32),
@@ -556,16 +606,16 @@
             pltpu.VMEM((8, 2, 256), F32),
             pltpu.VMEM((2, 25, 8, 128), F32),
             pltpu.VMEM((8, 512), F32),
-            pltpu.VMEM((384, 2048), BF16),
-            pltpu.VMEM((64, 256), BF16),
-            pltpu.VMEM((8, 64, 256), F32),
+            pltpu.VMEM((768, 1024), BF16),
+            pltpu.VMEM((128, 256), BF16),
+            pltpu.VMEM((3, 448, 256), F32),
             pltpu.VMEM((2048, 256), BF16),
             pltpu.VMEM((2048, 256), BF16),
             pltpu.VMEM((2048, 128), BF16),
             pltpu.VMEM((2048, 128), BF16),
             pltpu.VMEM((384, 512), BF16),
             pltpu.VMEM((384, 512), BF16),
-            pltpu.SemaphoreType.DMA((10,)),
+            pltpu.SemaphoreType.DMA((17,)),
             pltpu.SemaphoreType.DMA((4,)),
             pltpu.SemaphoreType.DMA((2,)),
             pltpu.SemaphoreType.DMA((2,)),
@@ -573,15 +623,18 @@
             pltpu.SemaphoreType.DMA((7, 2)),
             pltpu.SemaphoreType.DMA((COPIES,)),
             pltpu.SemaphoreType.DMA((COPIES,)),
+            pltpu.VMEM((2, 16, 128), F32),
+            pltpu.SemaphoreType.DMA((2,)),
+            pltpu.SemaphoreType.DMA((2,)),
         ],
         compiler_params=pltpu.CompilerParams(
-            collective_id=0, has_side_effects=True, vmem_limit_bytes=50 * 2**20
+            collective_id=0, has_side_effects=True, vmem_limit_bytes=60 * 2**20
         ),
     )(
         near_list,
         near_count,
         leaf_count,
-        mid_count,
+        mid_count.reshape(1, 1),
         leaf_list,
         mid_list,
         top_list.T,

time: 47.6 us -> 34.8 us (0.73)
  local copies, waits for them, and re-layouts: 11.4 us -> 0.61 us
  Pallas kernels: 35 us -> 33.4 us
    unnamed x29 -> x1, local copies, waits for them, and re-layouts: 11.4 us -> 0.61 us
    pallas_call x1, Pallas kernels: 35 us -> 33.4 us  [on_device(): pl.pallas_call(kernel, out_shape=pltpu.VMEM((8, 512), F32), in_specs=[hbm...]
where the time goes in v2:
time: 34.8 us; the launch traced here: 34.6 us
  Pallas kernels  33.4 us (96%)
  between operations  0.66 us (2%)
  local copies, waits for them, and re-layouts  0.61 us (2%)
    pallas_call x1, Pallas kernels, on_device(): pl.pallas_call(kernel, out_shape=pltpu.VMEM((8, 512), F32), in_specs=[hbm...  33.4 us

profile of v2, /device:TPU:1, one launch (start us, length us, event | category | flops | bytes accessed | tf_op | source)
XLA Modules:
  0.0 34.6 jit_solution(3065841317886399454)
XLA Ops:
  0.7 33.4 %shard_map.172 = f32[8,512]{1,0:T(8,128)S(1)} custom-call(s32[8,27]{1,0:T(8,128)} %near_list_hbm.1, s32[8]{0:T(128)} %near_count_hbm.1, s32[8]{0:T(128)} %leaf_count_hbm.1, s32[1,1]{1,0:T(1,128)} %bitcast.8.mid_count_hbm, s32[8,48]{1,0:T(8,128)} %leaf_list_hbm.1, s32[1,48]{1,0:T(1,128)} %mid_list_hbm.1, s32[16,32]{1,0:T(8,128)} %bitcast.13, f32[8,512]{1,0:T(8,128)} %x_hbm.1, ...), custom_call_target="tpu_custom_call" | custom-call | tf_op jit(solution)/shard_map/pallas_call | solution.py:581
  34.0 0.6 %copy.20 = f32[8,512]{1,0:T(8,128)} copy(f32[8,512]{1,0:T(8,128)S(1)} %shard_map.172) | data formatting | bytes 32768

commit v3 on v2

--- a/solution.py
+++ b/solution.py
@@ -16,7 +16,7 @@
 
 HALF = ROWS // 2
 U_ID, V_ID, W_ID = 0, 3, 15
-FORWARDED = 3
+FORWARDED = 0
 COPIES = 24
 
 
@@ -367,15 +367,14 @@
         sends.append(copy)
 
     def along_v(k, uu):
+        send(V_ID + 3 * k + 1, v, uu, dev_vp)
+        send(V_ID + 3 * k + 2, v, uu, dev_vm)
         if k >= FORWARDED:
             send(V_ID + 3 * k, v, uu, dev_v2)
-        send(V_ID + 3 * k + 1, v, uu, dev_vp)
-        send(V_ID + 3 * k + 2, v, uu, dev_vm)
-
-    send(U_ID, v, u, dev_u2)
+
     send(U_ID + 1, v, u, dev_up)
     send(U_ID + 2, v, u, dev_um)
-    along_v(0, u)
+    send(U_ID, v, u, dev_u2)
     list_copy().wait_recv()
     one_hot(1)
 
@@ -413,6 +412,8 @@
     for i in range(4):
         load_near[i].wait()
         near_pair(i)
+        if i == 3:
+            along_v(0, u)
 
     column(U_ID + 1, v, um, me).wait_recv()
     along_v(1, um)

time: 34.8 us -> 33.9 us (0.974)
  Pallas kernels: 33.4 us -> 32.5 us
    pallas_call x1, Pallas kernels: 33.4 us -> 32.5 us  [on_device(): pl.pallas_call(kernel, out_shape=pltpu.VMEM((8, 512), F32), in_specs=[hbm...]
where the time goes in v3:
time: 33.9 us; the launch traced here: 33.7 us
  Pallas kernels  32.5 us (96%)
  between operations  0.66 us (2%)
  local copies, waits for them, and re-layouts  0.61 us (2%)
    pallas_call x1, Pallas kernels, on_device(): pl.pallas_call(kernel, out_shape=pltpu.VMEM((8, 512), F32), in_specs=[hbm...  32.5 us

profile of v3, /device:TPU:1, one launch (start us, length us, event | category | flops | bytes accessed | tf_op | source)
XLA Modules:
  0.0 33.7 jit_solution(9885280754870635565)
XLA Ops:
  0.7 32.5 %shard_map.172 = f32[8,512]{1,0:T(8,128)S(1)} custom-call(s32[8,27]{1,0:T(8,128)} %near_list_hbm.1, s32[8]{0:T(128)} %near_count_hbm.1, s32[8]{0:T(128)} %leaf_count_hbm.1, s32[1,1]{1,0:T(1,128)} %bitcast.8.mid_count_hbm, s32[8,48]{1,0:T(8,128)} %leaf_list_hbm.1, s32[1,48]{1,0:T(1,128)} %mid_list_hbm.1, s32[16,32]{1,0:T(8,128)} %bitcast.13, f32[8,512]{1,0:T(8,128)} %x_hbm.1, ...), custom_call_target="tpu_custom_call" | custom-call | tf_op jit(solution)/shard_map/pallas_call | solution.py:582
  33.1 0.6 %copy.20 = f32[8,512]{1,0:T(8,128)} copy(f32[8,512]{1,0:T(8,128)S(1)} %shard_map.172) | data formatting | bytes 32768

commit v4 on v3

--- a/solution.py
+++ b/solution.py
@@ -15,6 +15,8 @@
 ROWS = 80
 
 HALF = ROWS // 2
+REL_U, REL_V, REL_SIB, REL_RIGHT, REL_LEFT = 8, 11, 14, 15, 16
+RELATIONS = 17
 U_ID, V_ID, W_ID = 0, 3, 15
 FORWARDED = 0
 COPIES = 24
@@ -115,6 +117,7 @@
     wanted_rows,
     swap_send,
     swap_recv,
+    ready_sem,
 ):
     me = lax.axis_index("cluster")
     c = lax.rem(me, 2)
@@ -142,17 +145,47 @@
     load_lin = load(1, lin_hbm, lin_v)
     load_lup = load(2, lup_hbm, lup_v)
     load_mup = load(3, mup_hbm, mup_v)
+    up, um, u2 = mod(u + 1, 4), mod(u - 1, 4), mod(u + 2, 4)
+    vp, vm, v2 = mod(v + 1, 4), mod(v - 1, 4), mod(v + 2, 4)
+    dev_up, dev_um, dev_u2 = device(v, up, z), device(v, um, z), device(v, u2, z)
+    dev_vp, dev_vm, dev_v2 = device(vp, u, z), device(vm, u, z), device(v2, u, z)
+
+    def rank(dev):
+        xx = lax.div(dev, 2 * Z * Y)
+        yy = lax.rem(lax.div(dev, 2 * Z), Y)
+        zz = lax.rem(lax.div(dev, 2), Z)
+        return ((zz * Y + yy) * X + xx) * 2 + lax.rem(dev, 2)
+
+    mine = rank(me)
+    relations = [
+        (REL_U, dev_u2, REL_U),
+        (REL_U + 1, dev_up, REL_U + 2),
+        (REL_U + 2, dev_um, REL_U + 1),
+        (REL_V, dev_v2, REL_V),
+        (REL_V + 1, dev_vp, REL_V + 2),
+        (REL_V + 2, dev_vm, REL_V + 1),
+        (REL_SIB, sibling, REL_SIB),
+        (REL_RIGHT, right, REL_LEFT),
+        (REL_LEFT, left, REL_RIGHT),
+    ]
+    relations += [(k, device(v, u, mod(z + k, Z)), Z - k) for k in range(1, Z)]
+    relations = [(i, dev, rank(dev), back) for i, dev, back in relations]
     barrier = pltpu.get_barrier_semaphore()
-    partners = [device(v, u, mod(z + k, Z)) for k in range(1, Z)]
-    up, um = mod(u + 1, 4), mod(u - 1, 4)
-    vp, vm = mod(v + 1, 4), mod(v - 1, 4)
-    dev_up, dev_um = device(v, up, z), device(v, um, z)
-    dev_vp, dev_vm = device(vp, u, z), device(vm, u, z)
-    u2, v2 = mod(u + 2, 4), mod(v + 2, 4)
-    dev_u2, dev_v2 = device(v, u2, z), device(v2, u, z)
-    partners += [dev_up, dev_um, dev_u2, dev_vp, dev_vm, dev_v2, sibling, right, left]
-    for partner in partners:
-        pl.semaphore_signal(barrier, inc=1, device_id=(partner,), device_id_type=MESH)
+    greetings = jnp.int32(0)
+    for _, dev, theirs, _ in relations:
+        greetings += (theirs < mine).astype(jnp.int32)
+
+        @pl.when(mine < theirs)
+        def _():
+            pl.semaphore_signal(barrier, inc=1, device_id=(dev,), device_id_type=MESH)
+
+    def ready(relation):
+        for i, _, theirs, _ in relations:
+            if i == relation:
+
+                @pl.when(mine < theirs)
+                def _():
+                    pl.semaphore_wait(ready_sem.at[i], 1)
 
     load_x.wait()
     load_lin.wait()
@@ -197,7 +230,17 @@
     my_rows = pl.ds(pl.multiple_of(z * 8, 8), 8)
     coef[c, v, u, my_rows, :] = flat(r)
 
-    pl.semaphore_wait(barrier, len(partners))
+    @pl.when(greetings > 0)
+    def _():
+        pl.semaphore_wait(barrier, greetings)
+
+    for _, dev, theirs, back in relations:
+
+        @pl.when(theirs < mine)
+        def _():
+            pl.semaphore_signal(
+                ready_sem.at[back], inc=1, device_id=(dev,), device_id_type=MESH
+            )
 
     def halo(i, source, target, dev):
         return pltpu.make_async_remote_copy(
@@ -229,17 +272,35 @@
             ),
         )
 
-    order = [4, 3, 5, 2, 6, 1, 7]
+    halo_to = ((right, rank(right)), (left, rank(left)))
+    for i, (dev, theirs) in enumerate(halo_to):
+
+        @pl.when(theirs < mine)
+        def _():
+            halo(i, 1, 2 * i, dev).start()
+
+    def to_plane(zz):
+        k = mod(zz - z, Z)
+
+        @pl.when(zz > z)
+        def _():
+            pl.semaphore_wait(ready_sem.at[k], 1)
+
+        @pl.when(zz != z)
+        def _():
+            for copy in along_z(k, z, device(v, u, zz)):
+                copy.start()
+
+    def from_plane(zz):
+        @pl.when(zz != z)
+        def _():
+            for copy in along_z(mod(z - zz, Z), zz, me):
+                copy.wait_recv()
+
+    stage[z] = flat(product(r, both_up))
     sends = []
-    for k in order:
-        copy = along_z(k - 1, z, device(v, u, mod(z + k, Z)))[0]
-        copy.start()
-        sends.append(copy)
-    stage[z] = flat(product(r, both_up))
-    for k in order:
-        copy = along_z(k - 1, z, device(v, u, mod(z + k, Z)))[1]
-        copy.start()
-        sends.append(copy)
+    for zz in range(Z):
+        to_plane(zz)
     load_lists = [
         load(10, leaf_count_hbm, leaf_count),
         load(11, mid_count_hbm, mid_count),
@@ -262,11 +323,6 @@
     load_mdn = load(7, mdn_hbm, mdn_v)
     load_ldn = load(8, ldn_hbm, ldn_v)
     load_lout = load(9, lout_hbm, lout_v)
-
-    halo_copies = [halo(0, 1, 0, right), halo(1, 1, 2, left)]
-    for copy in halo_copies:
-        copy.start()
-    sends += halo_copies
 
     def place(s, shift):
         cc = (s >> shift) & 1
@@ -338,13 +394,18 @@
     for copy in load_lists:
         copy.wait()
     slots()
+    ready(REL_SIB)
     list_copy().start()
     one_hot(0)
-
-    for k in order:
-        zz = mod(z - k, Z)
-        for copy in along_z(k - 1, zz, me):
-            copy.wait_recv()
+    for i, (dev, theirs) in enumerate(halo_to):
+
+        @pl.when(mine < theirs)
+        def _():
+            pl.semaphore_wait(ready_sem.at[REL_RIGHT + i], 1)
+            halo(i, 1, 2 * i, dev).start()
+
+    for zz in range(Z):
+        from_plane(zz)
     coef[c, v, u, 64:72, :] = stage[:, 0, :]
     coef[c, v, u, 72:80, :] = stage[:, 1, :]
 
@@ -372,6 +433,8 @@
         if k >= FORWARDED:
             send(V_ID + 3 * k, v, uu, dev_v2)
 
+    for i in range(3):
+        ready(REL_U + i)
     send(U_ID + 1, v, u, dev_up)
     send(U_ID + 2, v, u, dev_um)
     send(U_ID, v, u, dev_u2)
@@ -412,9 +475,10 @@
     for i in range(4):
         load_near[i].wait()
         near_pair(i)
-        if i == 3:
-            along_v(0, u)
-
+
+    for i in range(3):
+        ready(REL_V + i)
+    along_v(0, u)
     column(U_ID + 1, v, um, me).wait_recv()
     along_v(1, um)
     column(U_ID + 2, v, up, me).wait_recv()
@@ -555,6 +619,11 @@
 
     for copy in sends + [list_copy(), swap()]:
         copy.wait_send()
+    for i in range(2):
+        halo(i, 1, 2 * i, me).wait_send()
+    for k in range(1, Z):
+        for copy in along_z(k, z, me):
+            copy.wait_send()
 
 
 def on_device(
@@ -620,13 +689,14 @@
             pltpu.SemaphoreType.DMA((4,)),
             pltpu.SemaphoreType.DMA((2,)),
             pltpu.SemaphoreType.DMA((2,)),
-            pltpu.SemaphoreType.DMA((7, 2)),
-            pltpu.SemaphoreType.DMA((7, 2)),
+            pltpu.SemaphoreType.DMA((Z, 2)),
+            pltpu.SemaphoreType.DMA((Z, 2)),
             pltpu.SemaphoreType.DMA((COPIES,)),
             pltpu.SemaphoreType.DMA((COPIES,)),
             pltpu.VMEM((2, 16, 128), F32),
             pltpu.SemaphoreType.DMA((2,)),
             pltpu.SemaphoreType.DMA((2,)),
+            pltpu.SemaphoreType.REGULAR((RELATIONS,)),
         ],
         compiler_params=pltpu.CompilerParams(
             collective_id=0, has_side_effects=True, vmem_limit_bytes=60 * 2**20

time: 33.9 us -> 33.5 us (0.988)
  Pallas kernels: 32.5 us -> 32 us
    pallas_call x1, Pallas kernels: 32.5 us -> 32 us  [on_device(): pl.pallas_call(kernel, out_shape=pltpu.VMEM((8, 512), F32), in_specs=[hbm...]
where the time goes in v4:
time: 33.5 us; the launch traced here: 33.3 us
  Pallas kernels  32 us (96%)
  between operations  0.66 us (2%)
  local copies, waits for them, and re-layouts  0.61 us (2%)
    pallas_call x1, Pallas kernels, on_device(): pl.pallas_call(kernel, out_shape=pltpu.VMEM((8, 512), F32), in_specs=[hbm...  32 us

profile of v4, /device:TPU:1, one launch (start us, length us, event | category | flops | bytes accessed | tf_op | source)
XLA Modules:
  0.0 33.3 jit_solution(13988392678631644065)
XLA Ops:
  0.7 32.0 %shard_map.172 = f32[8,512]{1,0:T(8,128)S(1)} custom-call(s32[8,27]{1,0:T(8,128)} %near_list_hbm.1, s32[8]{0:T(128)} %near_count_hbm.1, s32[8]{0:T(128)} %leaf_count_hbm.1, s32[1,1]{1,0:T(1,128)} %bitcast.8.mid_count_hbm, s32[8,48]{1,0:T(8,128)} %leaf_list_hbm.1, s32[1,48]{1,0:T(1,128)} %mid_list_hbm.1, s32[16,32]{1,0:T(8,128)} %bitcast.13, f32[8,512]{1,0:T(8,128)} %x_hbm.1, ...), custom_call_target="tpu_custom_call" | custom-call | tf_op jit(solution)/shard_map/pallas_call | solution.py:651
  32.7 0.6 %copy.20 = f32[8,512]{1,0:T(8,128)} copy(f32[8,512]{1,0:T(8,128)S(1)} %shard_map.172) | data formatting | bytes 32768

commit v5 on v4

--- a/solution.py
+++ b/solution.py
@@ -14,12 +14,12 @@
 X, Y, Z = 4, 4, 8
 ROWS = 80
 
-HALF = ROWS // 2
+EARLY = 4
+PARTS = (pl.ds(0, 8 * EARLY), pl.ds(8 * EARLY, ROWS - 8 * EARLY), pl.ds(0, ROWS))
+U_ID, V_ID = 0, 3
+COPIES = 15
 REL_U, REL_V, REL_SIB, REL_RIGHT, REL_LEFT = 8, 11, 14, 15, 16
 RELATIONS = 17
-U_ID, V_ID, W_ID = 0, 3, 15
-FORWARDED = 0
-COPIES = 24
 
 
 def mod(a, n):
@@ -124,12 +124,13 @@
     z = lax.rem(lax.div(me, 2), Z)
     y = lax.rem(lax.div(me, 2 * Z), Y)
     x = lax.div(me, 2 * Z * Y)
-    v = x + c * (y - x)
-    u = y + c * (x - y)
+    flip = 1 - c
+    v = x + flip * (y - x)
+    u = y + flip * (x - y)
 
     def device(vv, uu, zz):
-        xx = vv + c * (uu - vv)
-        yy = uu + c * (vv - uu)
+        xx = vv + flip * (uu - vv)
+        yy = uu + flip * (vv - uu)
         return ((xx * Y + yy) * Z + zz) * 2 + c
 
     sibling = me + 1 - 2 * c
@@ -291,11 +292,10 @@
             for copy in along_z(k, z, device(v, u, zz)):
                 copy.start()
 
-    def from_plane(zz):
+    def from_plane(zz, part):
         @pl.when(zz != z)
         def _():
-            for copy in along_z(mod(z - zz, Z), zz, me):
-                copy.wait_recv()
+            along_z(mod(z - zz, Z), zz, me)[part].wait_recv()
 
     stage[z] = flat(product(r, both_up))
     sends = []
@@ -324,13 +324,53 @@
     load_ldn = load(8, ldn_hbm, ldn_v)
     load_lout = load(9, lout_hbm, lout_v)
 
+    def column(part, i, vv, uu, dev):
+        ref = coef.at[c, vv, uu, PARTS[part]]
+        sems = min(part, 1)
+        return pltpu.make_async_remote_copy(
+            src_ref=ref,
+            dst_ref=ref,
+            send_sem=col_send.at[sems, i],
+            recv_sem=col_recv.at[sems, i],
+            device_id=(dev,),
+            device_id_type=MESH,
+        )
+
+    def along_u(part):
+        for i, dev in ((1, dev_up), (2, dev_um), (0, dev_u2)):
+            column(part, U_ID + i, v, u, dev).start()
+
+    def along_v(part, k, uu):
+        for i, dev in ((1, dev_vp), (2, dev_vm), (0, dev_v2)):
+            column(part, V_ID + 3 * k + i, v, uu, dev).start()
+
+    def turn(part):
+        for k, i, uu in ((1, 1, um), (2, 2, up), (3, 0, u2)):
+            column(part, U_ID + i, v, uu, me).wait_recv()
+            along_v(part, k, uu)
+
+    def from_v(part, k, uu):
+        for i, vv in ((1, vm), (2, vp), (0, v2)):
+            column(part, V_ID + 3 * k + i, vv, uu, me).wait_recv()
+
+    def by_plane(step, first=None):
+        @pl.when(z < EARLY)
+        def _():
+            if first is not None:
+                first()
+            step(1)
+
+        @pl.when(z >= EARLY)
+        def _():
+            step(2)
+
     def place(s, shift):
         cc = (s >> shift) & 1
         zz = (s >> (shift + 1)) & 7
         yy = (s >> (shift + 4)) & 3
         xx = (s >> (shift + 6)) & 3
-        vv = jnp.where(cc == 0, xx, yy)
-        uu = jnp.where(cc == 0, yy, xx)
+        vv = jnp.where(cc == 1, xx, yy)
+        uu = jnp.where(cc == 1, yy, xx)
         return cc, uu * 32 + vv * 8 + zz
 
     def live_of(counts, width):
@@ -383,8 +423,8 @@
         wanted = jnp.sum(wanted.astype(F32), axis=1, keepdims=True)
         k = iota((16, 256), 1)
         uu, vv = (k >> 6) & 3, (k >> 4) & 3
-        xx = vv + c * (uu - vv)
-        yy = uu + c * (vv - uu)
+        xx = vv + flip * (uu - vv)
+        yy = uu + flip * (vv - uu)
         top = (xx * 4 + yy) * 2 + ((k & 7) >> 2)
         top = jnp.where((k & 8) == 8, top, -1).astype(F32)
         onehot2[side * 64 + 48 : side * 64 + 64, :] = jnp.where(
@@ -404,40 +444,23 @@
             pl.semaphore_wait(ready_sem.at[REL_RIGHT + i], 1)
             halo(i, 1, 2 * i, dev).start()
 
+    for i in range(3):
+        ready(REL_U + i)
+    for zz in range(EARLY):
+        from_plane(zz, 0)
+
+    @pl.when(z < EARLY)
+    def _():
+        along_u(0)
+
+    for zz in range(EARLY, Z):
+        from_plane(zz, 0)
     for zz in range(Z):
-        from_plane(zz)
+        from_plane(zz, 1)
     coef[c, v, u, 64:72, :] = stage[:, 0, :]
     coef[c, v, u, 72:80, :] = stage[:, 1, :]
 
-    def column(i, vv, uu, dev, half=None):
-        ref = coef.at[c, vv, uu]
-        if half is not None:
-            ref = coef.at[c, vv, uu, pl.ds(half * HALF, HALF)]
-        return pltpu.make_async_remote_copy(
-            src_ref=ref,
-            dst_ref=ref,
-            send_sem=col_send.at[i],
-            recv_sem=col_recv.at[i],
-            device_id=(dev,),
-            device_id_type=MESH,
-        )
-
-    def send(i, vv, uu, dev, half=None):
-        copy = column(i, vv, uu, dev, half)
-        copy.start()
-        sends.append(copy)
-
-    def along_v(k, uu):
-        send(V_ID + 3 * k + 1, v, uu, dev_vp)
-        send(V_ID + 3 * k + 2, v, uu, dev_vm)
-        if k >= FORWARDED:
-            send(V_ID + 3 * k, v, uu, dev_v2)
-
-    for i in range(3):
-        ready(REL_U + i)
-    send(U_ID + 1, v, u, dev_up)
-    send(U_ID + 2, v, u, dev_um)
-    send(U_ID, v, u, dev_u2)
+    by_plane(along_u)
     list_copy().wait_recv()
     one_hot(1)
 
@@ -478,13 +501,13 @@
 
     for i in range(3):
         ready(REL_V + i)
-    along_v(0, u)
-    column(U_ID + 1, v, um, me).wait_recv()
-    along_v(1, um)
-    column(U_ID + 2, v, up, me).wait_recv()
-    along_v(2, up)
-    column(U_ID, v, u2, me).wait_recv()
-    along_v(3, u2)
+
+    def early_v():
+        along_v(0, 0, u)
+        turn(0)
+
+    by_plane(lambda part: along_v(part, 0, u), early_v)
+    by_plane(turn)
 
     load_leaf.wait()
     load_mid.wait()
@@ -569,18 +592,7 @@
         )
 
     for k, uu in enumerate([u, um, up, u2]):
-        column(V_ID + 3 * k + 1, vm, uu, me).wait_recv()
-        if k < FORWARDED:
-            send(W_ID + 2 * k, vm, uu, dev_vp, 0)
-        column(V_ID + 3 * k + 2, vp, uu, me).wait_recv()
-        if k < FORWARDED:
-            send(W_ID + 2 * k + 1, vp, uu, dev_vm, 1)
-    for k, uu in enumerate([u, um, up, u2]):
-        if k < FORWARDED:
-            column(W_ID + 2 * k, v2, uu, me, 0).wait_recv()
-            column(W_ID + 2 * k + 1, v2, uu, me, 1).wait_recv()
-        else:
-            column(V_ID + 3 * k, v2, uu, me).wait_recv()
+        by_plane(lambda part: from_v(part, k, uu), lambda: from_v(0, k, uu))
         if k < 3:
             plane(uu, 1, k == 0)
             plane(uu, 0, k == 0)
@@ -619,6 +631,12 @@
 
     for copy in sends + [list_copy(), swap()]:
         copy.wait_send()
+
+    def sent(part):
+        for i in range(COPIES):
+            column(part, i, v, u, me).wait_send()
+
+    by_plane(sent, lambda: sent(0))
     for i in range(2):
         halo(i, 1, 2 * i, me).wait_send()
     for k in range(1, Z):
@@ -691,8 +709,8 @@
             pltpu.SemaphoreType.DMA((2,)),
             pltpu.SemaphoreType.DMA((Z, 2)),
             pltpu.SemaphoreType.DMA((Z, 2)),
-            pltpu.SemaphoreType.DMA((COPIES,)),
-            pltpu.SemaphoreType.DMA((COPIES,)),
+            pltpu.SemaphoreType.DMA((2, COPIES)),
+            pltpu.SemaphoreType.DMA((2, COPIES)),
             pltpu.VMEM((2, 16, 128), F32),
             pltpu.SemaphoreType.DMA((2,)),
             pltpu.SemaphoreType.DMA((2,)),

time: 33.5 us -> 33.2 us (level)
  no operation moved by 1% of the time
where the time goes in v5:
time: 33.2 us; the launch traced here: 33 us
  Pallas kernels  31.7 us (95%)
  between operations  0.66 us (2%)
  local copies, waits for them, and re-layouts  0.61 us (2%)
    pallas_call x1, Pallas kernels, on_device(): pl.pallas_call(kernel, out_shape=pltpu.VMEM((8, 512), F32), in_specs=[hbm...  31.7 us

profile of v5, /device:TPU:1, one launch (start us, length us, event | category | flops | bytes accessed | tf_op | source)
XLA Modules:
  0.0 33.0 jit_solution(16165410433582988176)
XLA Ops:
  0.7 31.7 %shard_map.172 = f32[8,512]{1,0:T(8,128)S(1)} custom-call(s32[8,27]{1,0:T(8,128)} %near_list_hbm.1, s32[8]{0:T(128)} %near_count_hbm.1, s32[8]{0:T(128)} %leaf_count_hbm.1, s32[1,1]{1,0:T(1,128)} %bitcast.8.mid_count_hbm, s32[8,48]{1,0:T(8,128)} %leaf_list_hbm.1, s32[1,48]{1,0:T(1,128)} %mid_list_hbm.1, s32[16,32]{1,0:T(8,128)} %bitcast.13, f32[8,512]{1,0:T(8,128)} %x_hbm.1, ...), custom_call_target="tpu_custom_call" | custom-call | tf_op jit(solution)/shard_map/pallas_call | solution.py:669
  32.4 0.6 %copy.20 = f32[8,512]{1,0:T(8,128)} copy(f32[8,512]{1,0:T(8,128)S(1)} %shard_map.172) | data formatting | bytes 32768

commit v6 on v5

--- a/solution.py
+++ b/solution.py
@@ -581,12 +581,13 @@
         rows = onehot2[side * 64 : (side + 1) * 64, :]
         picked[side, 384:448, :] = dot(rows, hi) + dot(rows, lo)
 
-    def swap():
+    def swap(part):
+        rows = pl.ds(192 * part, 192 + 64 * part)
         return pltpu.make_async_remote_copy(
-            src_ref=picked.at[1],
-            dst_ref=picked.at[2],
-            send_sem=swap_send.at[1],
-            recv_sem=swap_recv.at[1],
+            src_ref=picked.at[1, rows],
+            dst_ref=picked.at[2, rows],
+            send_sem=swap_send.at[1 + part],
+            recv_sem=swap_recv.at[1 + part],
             device_id=(sibling,),
             device_id_type=MESH,
         )
@@ -596,12 +597,14 @@
         if k < 3:
             plane(uu, 1, k == 0)
             plane(uu, 0, k == 0)
+    plane(u2, 1, False)
+    swap(0).start()
     upper(1)
-    plane(u2, 1, False)
-    swap().start()
+    swap(1).start()
     upper(0)
     plane(u2, 0, False)
-    swap().wait_recv()
+    swap(0).wait_recv()
+    swap(1).wait_recv()
     total = picked[0] + picked[2]
 
     gap = jnp.zeros((16, 256), F32)
@@ -629,7 +632,7 @@
     field = jnp.concatenate([far, high], axis=1)
     out_ref[...] = near_acc[...] + product2(field, ohi[...], olo[...])
 
-    for copy in sends + [list_copy(), swap()]:
+    for copy in sends + [list_copy(), swap(0), swap(1)]:
         copy.wait_send()
 
     def sent(part):
@@ -712,8 +715,8 @@
             pltpu.SemaphoreType.DMA((2, COPIES)),
             pltpu.SemaphoreType.DMA((2, COPIES)),
             pltpu.VMEM((2, 16, 128), F32),
-            pltpu.SemaphoreType.DMA((2,)),
-            pltpu.SemaphoreType.DMA((2,)),
+            pltpu.SemaphoreType.DMA((3,)),
+            pltpu.SemaphoreType.DMA((3,)),
             pltpu.SemaphoreType.REGULAR((RELATIONS,)),
         ],
         compiler_params=pltpu.CompilerParams(

time: 33.2 us -> 33.1 us (level)
  no operation moved by 1% of the time
where the time goes in v6:
time: 33.1 us; the launch traced here: 32.9 us
  Pallas kernels  31.6 us (95%)
  between operations  0.66 us (2%)
  local copies, waits for them, and re-layouts  0.61 us (2%)
    pallas_call x1, Pallas kernels, on_device(): pl.pallas_call(kernel, out_shape=pltpu.VMEM((8, 512), F32), in_specs=[hbm...  31.6 us

profile of v6, /device:TPU:1, one launch (start us, length us, event | category | flops | bytes accessed | tf_op | source)
XLA Modules:
  0.0 32.9 jit_solution(2374478336708504395)
XLA Ops:
  0.7 31.6 %shard_map.172 = f32[8,512]{1,0:T(8,128)S(1)} custom-call(s32[8,27]{1,0:T(8,128)} %near_list_hbm.1, s32[8]{0:T(128)} %near_count_hbm.1, s32[8]{0:T(128)} %leaf_count_hbm.1, s32[1,1]{1,0:T(1,128)} %bitcast.8.mid_count_hbm, s32[8,48]{1,0:T(8,128)} %leaf_list_hbm.1, s32[1,48]{1,0:T(1,128)} %mid_list_hbm.1, s32[16,32]{1,0:T(8,128)} %bitcast.13, f32[8,512]{1,0:T(8,128)} %x_hbm.1, ...), custom_call_target="tpu_custom_call" | custom-call | tf_op jit(solution)/shard_map/pallas_call | solution.py:672
  32.3 0.6 %copy.20 = f32[8,512]{1,0:T(8,128)} copy(f32[8,512]{1,0:T(8,128)S(1)} %shard_map.172) | data formatting | bytes 32768
